TPU v7x, 128 devices: a whole 4x4x4 slice. The times are simulated.
128 devices in a mesh: row: 16 (over x, y_lo, core), col: 8 (over z, y_hi).
Axes of the slice: x: 4, y: 4 (y_hi: 2, y_lo: 2; y = y_hi * 2 + y_lo), z: 4, core: 2. Of those that a mesh axis runs over, the one named last changes fastest.
Arguments:
- orbitals: bfloat16 [12288, 6144], P('col', 'row'), may hold values from -6 to 6
- fock_blocks: bfloat16 [65536, 1024], P(('row', 'col')), may hold values from -0.078125 to 0.078125
- fock_where: int32 [65536], P(('row', 'col')), may hold values from 0 to 1151, as said below
- density_blocks: bfloat16 [5120, 1024], P(('row', 'col')), may hold values from -6 to 6
- integrals: bfloat16 [1024, 1024, 1024], P(('row', 'col')), may hold values from -0.1875 to 0.1875
- quartet_density: int32 [1024], P(('row', 'col')), may hold values from 0 to 5119, as said below
- quartet_target: int32 [1024], P(('row', 'col')), may hold values from 0 to 4095, as said below
- quartet_count: int32 [128], P(('row', 'col')), may hold values from 1 to 8, as said below
Outputs:
- applied_fock: bfloat16 [12288, 6144], P('row', 'col')
Inputs may be any that keep to these rules, and one draw needn't show every extreme that they name: `fock_where`: within one device the positions are distinct, from 0 to 1151. `quartet_density`: A quartet held by a device in row r names a density block held by a device in row r - 1, r or r + 1 (cyclically over 16 rows); device d holds blocks d * 40 to d * 40 + 39. `quartet_target`: the value t names block t % 512 of the device in column t // 512 of the quartet's own row. `quartet_count`: some device holds 8 live quartets; live quartets are the first slots of a device.
All inputs are finite; a program needn't handle non-finite values.
Results may differ from a plain program's by a relative error of at most 0.02.
Values may be sent and summed in bfloat16 or wider, within the bound.
No kernel may reach another device: no remote copies, remote signals or barrier semaphores. Data moves between devices by JAX's collectives and lax.ppermute only.
A program may use at most 320 MiB of HBM per device.

v0:
```python
import functools

import jax
import jax.numpy as jnp
from jax import lax
from jax.experimental import pallas as pl
from jax.experimental.pallas import tpu as pltpu
from jax.sharding import PartitionSpec as P

BS = 32
TROWS, TCOLS = 24, 48
KCAP, PCAP, QCAP = 512, 40, 8
ROWS, COLS = TROWS * BS, TCOLS * BS
GROUPS = TCOLS // 4
EXT = 1024 + 128
W = 128
AXES = ("row", "col")
SLOT_A, SLOT_B = (1, 3, 0, 2), (0, 2, 1, 3)
MB = 1 << 20
bf16, f32 = jnp.bfloat16, jnp.float32


def coords(d):
    r, k = d // 8, d % 8
    return dict(x=r // 4, yl=r // 2 % 2, c=r % 2, z=k // 2, yh=k % 2)


def number(x, yl, c, z, yh):
    return ((x % 4) * 4 + yl * 2 + c) * 8 + (z % 4) * 2 + yh


def move(value, to):
    pairs = []
    for d in range(128):
        place = coords(d)
        target = dict(place)
        target.update(to(**place))
        pairs.append((d, number(**target)))
    return lax.ppermute(value, AXES, pairs)


def shift_x(value, by):
    return move(value, lambda x, **o: dict(x=x + by))


def shift_z(value, by):
    return move(value, lambda z, **o: dict(z=z + by))


def swap_z(value, by):
    return move(value, lambda z, **o: dict(z=z ^ by))


def swap_core(value):
    return move(value, lambda c, **o: dict(c=1 - c))


def swap_yh(value):
    return move(value, lambda yh, **o: dict(yh=1 - yh))


def shift_row(value, by):
    pairs = [(d, (d + 8 * by) % 128) for d in range(128)]
    return lax.ppermute(value, AXES, pairs)


def move_y(value, table):
    def to(yl, yh, **o):
        y = table[yh * 2 + yl]
        return dict(yl=y % 2, yh=y // 2)

    return move(value, to)


def here():
    r, k = lax.axis_index("row"), lax.axis_index("col")
    return dict(r=r, k=k, x=r // 4, yl=r // 2 % 2, c=r % 2, z=k // 2, yh=k % 2)


def call(kernel, out_shape, vmem, *, in_specs, after=(), gflop=0, **kw):
    n = len(after)
    run = pl.pallas_call(
        lambda *refs: kernel(*refs[n:]),
        out_shape=out_shape,
        in_specs=[ANY] * n + list(in_specs),
        compiler_params=pltpu.CompilerParams(vmem_limit_bytes=vmem * MB),
        cost_estimate=pl.CostEstimate(flops=gflop * 10**9 + 1, bytes_accessed=1, transcendentals=0),
        **kw,
    )
    return lambda *operands: run(*after, *operands)


VM = pl.BlockSpec(memory_space=pltpu.VMEM)
SM = pl.BlockSpec(memory_space=pltpu.SMEM)
ANY = pl.BlockSpec(memory_space=pl.ANY)


def select_kernel(req_own, req_a, req_b, p0, p1, p2, p3, out_own, out_a, out_b):
    at = here()
    parts = (p0, p1, p2, p3)
    steps = (0, 3, 1, 2)
    span = 2 * PCAP
    lane = lax.broadcasted_iota(jnp.int32, (16, span), 1)
    row = lax.broadcasted_iota(jnp.int32, (16, span), 0)
    for req, out in ((req_own, out_own), (req_a, out_a), (req_b, out_b)):
        want = jnp.full((16, span), -1, jnp.int32)
        for q in range(QCAP):
            want = jnp.where(row == q, req[q], want)
        total = jnp.zeros((16, 1024), f32)
        for part, step in zip(parts, steps):
            z = (at["z"] + step) % 4
            yh = jnp.where(lane < PCAP, at["yh"], 1 - at["yh"])
            held = (at["r"] * 8 + z * 2 + yh) * PCAP + jnp.where(lane < PCAP, lane, lane - PCAP)
            hot = (want == held).astype(f32).astype(bf16)
            total = total + jnp.dot(hot, part[...], preferred_element_type=f32)
        out[...] = total.astype(bf16)


def select(requests, parts):
    shape = jax.ShapeDtypeStruct((16, 1024), bf16)
    return call(
        select_kernel,
        (shape,) * 3,
        6,
        in_specs=[SM] * 3 + [VM] * 4,
        out_specs=[VM] * 3,
    )(*requests, *parts)


def terms_kernel(count, target, v0, v1, v2, integral, out, buf, sems):
    def fetch(q):
        return pltpu.make_async_copy(integral.at[q], buf.at[q], sems.at[q])

    for q in range(QCAP):
        fetch(q).start()
    out[...] = jnp.zeros_like(out)
    col = lax.broadcasted_iota(jnp.int32, (QCAP, 128), 1)
    row = lax.broadcasted_iota(jnp.int32, (QCAP, 128), 0)
    mark = jnp.zeros((QCAP, 128), jnp.int32)
    core = here()["c"]
    for i in range(QCAP):
        t = target[i]
        note = jnp.where(col == 0, t // KCAP, jnp.where(col == 1, t % KCAP // 32, jnp.where(col == 2, t % 32, core)))
        mark = jnp.where(row == i, note, mark)
    out[:, 1024:EXT] = mark.astype(f32).astype(bf16)
    v = v0[...].astype(f32) + v1[...].astype(f32) + v2[...].astype(f32)
    rows = lax.broadcasted_iota(jnp.int32, (16, 1024), 0)
    places = lax.broadcasted_iota(jnp.int32, (QCAP, 1024), 0)

    def one(q, carry):
        fetch(q).wait()
        vector = jnp.sum(jnp.where(rows == q, v, 0.0), axis=0, keepdims=True)
        sums = []
        for h in range(2):
            acc = jnp.zeros((512, 128), f32)
            for a in range(8):
                lanes = slice(a * 128, (a + 1) * 128)
                acc = acc + buf[q, h * 512 : (h + 1) * 512, lanes].astype(f32) * vector[:, lanes]
            sums.append(jnp.sum(acc.T, axis=0, keepdims=True))
        term = jnp.where(q < count[0], jnp.concatenate(sums, axis=1), 0.0)
        out[:, 0:1024] = jnp.where(places == q, term, out[:, 0:1024].astype(f32)).astype(bf16)
        return carry

    lax.fori_loop(0, QCAP, one, 0)


def exchange(count, target, vectors, integrals):
    return call(
        terms_kernel,
        jax.ShapeDtypeStruct((QCAP, EXT), bf16),
        48,
        in_specs=[SM, SM, VM, VM, VM, ANY],
        out_specs=VM,
        scratch_shapes=[pltpu.VMEM((QCAP, 1024, 1024), bf16), pltpu.SemaphoreType.DMA((QCAP,))],
    )(count, target, *vectors, integrals)


def tiles_kernel(near, f0, f1, t0, t1, out, f, tcur, wide, spread):
    g = pl.program_id(0)
    at = here()
    for i, stored in enumerate((f0, f1)):

        @pl.when(g == i)
        def _():
            f[...] = stored[...]

    @pl.when(g == 0)
    def _():
        for i, t in enumerate((t0, t1)):
            tcur[64 * i : 64 * i + 64, :] = t[...]

    k = at["z"] * 2 + (at["yh"] if near else 1 - at["yh"])
    marks = tcur[:, 1024:EXT].astype(f32)
    slot = (marks[:, 1:2] * 32.0 + marks[:, 2:3]).astype(jnp.int32)
    core = jnp.where(g == 0, at["c"], 1 - at["c"])
    slot = jnp.where(marks[:, 0:1].astype(jnp.int32) == k, slot, -1)
    slot = jnp.where(marks[:, 3:4].astype(jnp.int32) == core, slot, -1)
    spots = lax.broadcasted_iota(jnp.int32, (128, KCAP), 1)
    hot = (slot == spots).astype(f32).astype(bf16)
    update = lax.dot_general(hot, tcur[:, 0:1024], (((0,), (0,)), ((), ())), preferred_element_type=f32)
    fock = (f[:KCAP, :].astype(f32) + 0.25 * update).astype(bf16)
    place = f[KCAP:, :KCAP].astype(f32).T
    tr = place[:, 0:1].astype(jnp.int32)
    tc = place[:, 1:2].astype(jnp.int32)
    lane = lax.broadcasted_iota(jnp.int32, (KCAP, 512), 1)
    keep = (lane % 128 // BS) == (tc % 4)
    src = lax.broadcasted_iota(jnp.int32, (128, 512), 0)
    dst = lax.broadcasted_iota(jnp.int32, (128, 512), 1)
    copy = (src == dst // 128 * BS + dst % BS).astype(f32).astype(bf16)
    for a in range(8):
        piece = jnp.dot(fock[:, a * 128 : (a + 1) * 128], copy, preferred_element_type=f32)
        wide[:, a * 512 : (a + 1) * 512] = jnp.where(keep, piece, 0.0).astype(bf16)
    spot = lax.broadcasted_iota(jnp.int32, (KCAP, GROUPS * TROWS), 1)
    put = (spot == tc // 4 * TROWS + tr).astype(f32).astype(bf16)
    for h in range(8):
        spread[...] = lax.dot_general(
            put, wide[:, h * 512 : (h + 1) * 512], (((0,), (0,)), ((), ())), preferred_element_type=f32
        )
        for p in range(2):
            for t in range(GROUPS):
                pair = [
                    spread[t * TROWS : (t + 1) * TROWS, (2 * p + o) * 128 : (2 * p + o + 1) * 128]
                    for o in range(2)
                ]
                start = (4 * h + 2 * p) * TROWS
                out[start : start + 2 * TROWS, t * 128 : (t + 1) * 128] = jnp.concatenate(pair, axis=0).astype(bf16)


def tiles(near, focks, terms, after, gflop=0):
    return call(
        functools.partial(tiles_kernel, near),
        jax.ShapeDtypeStruct((2 * ROWS, COLS), bf16),
        24,
        after=after,
        gflop=gflop,
        grid=(2,),
        in_specs=[VM] * 4,
        out_specs=pl.BlockSpec((ROWS, COLS), lambda g: (g, 0)),
        scratch_shapes=[
            pltpu.VMEM((KCAP + 16, 1024), bf16),
            pltpu.VMEM((128, EXT), bf16),
            pltpu.VMEM((KCAP, 4096), bf16),
            pltpu.VMEM((GROUPS * TROWS, 512), f32),
        ],
    )(*focks, *terms)


def pack_kernel(blocks, where, out):
    out[:KCAP, :] = blocks[...]
    spot = jnp.concatenate([where[j : j + 1, :] for j in range(KCAP // 128)], axis=1)
    row = lax.broadcasted_iota(jnp.int32, (16, KCAP), 0)
    note = jnp.where(row == 0, spot // TCOLS, jnp.where(row == 1, spot % TCOLS, 0))
    out[KCAP:, :KCAP] = note.astype(f32).astype(bf16)
    out[KCAP:, KCAP:] = jnp.zeros((16, 1024 - KCAP), bf16)


def pack(blocks, where):
    return call(
        pack_kernel,
        jax.ShapeDtypeStruct((KCAP + 16, 1024), bf16),
        8,
        in_specs=[VM] * 2,
        out_specs=VM,
    )(blocks, where.reshape(KCAP // 128, 128))


def hold_kernel(start, value, out, sem):
    copy = pltpu.make_async_copy(value.at[start : start + out.shape[0]], out, sem)
    copy.start()
    copy.wait()


def hold(value, after, start=0, rows=None):
    return call(
        functools.partial(hold_kernel, start),
        jax.ShapeDtypeStruct((rows or value.shape[0], *value.shape[1:]), value.dtype),
        2,
        after=after,
        in_specs=[ANY],
        out_specs=ANY,
        scratch_shapes=[pltpu.SemaphoreType.DMA],
    )(value)


def cut_kernel(j, value, out, sem):
    copy = pltpu.make_async_copy(value.at[:, j * W : (j + 1) * W], out, sem)
    copy.start()
    copy.wait()


def cut(value, j, after):
    return call(
        functools.partial(cut_kernel, j),
        jax.ShapeDtypeStruct((COLS, W), bf16),
        2,
        after=after,
        in_specs=[ANY],
        out_specs=ANY,
        scratch_shapes=[pltpu.SemaphoreType.DMA],
    )(value)


def join_kernel(a, b, out, sems):
    copies = [pltpu.make_async_copy(src, out.at[i * COLS : (i + 1) * COLS], sems.at[i]) for i, src in enumerate((a, b))]
    for copy in copies:
        copy.start()
    for copy in copies:
        copy.wait()


def join(a, b, after):
    return call(
        join_kernel,
        jax.ShapeDtypeStruct((2 * COLS, W), bf16),
        2,
        after=after,
        in_specs=[ANY] * 2,
        out_specs=ANY,
        scratch_shapes=[pltpu.SemaphoreType.DMA((2,))],
    )(a, b)


def turned(orbitals, j, after):
    piece = cut(orbitals, j, after)
    return move_y(piece, SLOT_A), move_y(piece, SLOT_B)


def product_kernel(sizes, steps, near, far, *refs):
    at = here()
    n = len(sizes)
    wide = n * W
    blocks, outs, cols, sems = refs[: sum(sizes)], refs[sum(sizes) : -2], refs[-2], refs[-1]
    first = jnp.where(at["yh"] == at["yl"], COLS, 0)
    copies = []
    base = 0
    for j, size in enumerate(sizes):
        plan = [(b, s, h, h * COLS) for b, s in ((0, 0), (1, 3), (2, 1)) for h in range(2)]
        if size == 4:
            plan += [(3, 2, 0, 0), (3, 2, 1, COLS)]
        else:
            plan += [(3, 2, 0, 0), (4, 2, 1, 0)]
        for b, step, slot, start in plan:
            to = (at["x"] + step - at["z"] + 4) % 4
            wanted, place = to == steps[0], 0
            for i, other in enumerate(steps[1:]):
                wanted = jnp.logical_or(wanted, to == other)
                place = jnp.where(to == other, i + 1, place)
            lane = pl.multiple_of((place * n + j) * W, W)
            row = pl.multiple_of(first if slot == 0 else COLS - first, COLS)
            dst = cols.at[pl.ds(row, COLS), pl.ds(lane, W)]
            copy = pltpu.make_async_copy(blocks[base + b].at[start : start + COLS], dst, sems.at[len(copies)])
            copies.append((wanted, copy))
        base += size
    for wanted, copy in copies:

        @pl.when(wanted)
        def _():
            copy.start()

    for wanted, copy in copies:

        @pl.when(wanted)
        def _():
            copy.wait()

    for i in range(2):
        rows = slice(i * ROWS, (i + 1) * ROWS)
        part = jnp.dot(near[rows, :], cols[:COLS, :], preferred_element_type=f32)
        part = (part + jnp.dot(far[rows, :], cols[COLS:, :], preferred_element_type=f32)).astype(bf16)
        for o, out in enumerate(outs):
            out[rows, :] = part[:, o * wide : (o + 1) * wide]


def product(mats, chunks, steps, after=(), gflop=0):
    n = len(chunks)
    sizes = tuple(len(c) for c in chunks)
    return call(
        functools.partial(product_kernel, sizes, steps),
        (jax.ShapeDtypeStruct((2 * ROWS, n * W), bf16),) * len(steps),
        24,
        after=after,
        gflop=gflop,
        in_specs=[VM] * 2 + [ANY] * sum(sizes),
        out_specs=[VM] * len(steps),
        scratch_shapes=[pltpu.VMEM((2 * COLS, len(steps) * n * W), bf16), pltpu.SemaphoreType.DMA((8 * n,))],
    )(*mats, *(b for c in chunks for b in c))


def merge_kernel(pp, pm, above, below, pp_out, pm_out):
    pp_out[:ROWS, :] = (pp[:ROWS, :].astype(f32) + above[...].astype(f32)).astype(bf16)
    pp_out[ROWS:, :] = pp[ROWS:, :]
    pm_out[:ROWS, :] = pm[:ROWS, :]
    pm_out[ROWS:, :] = (pm[ROWS:, :].astype(f32) + below[...].astype(f32)).astype(bf16)


def merge(pp, pm, above, below, after):
    shape = jax.ShapeDtypeStruct(pp.shape, bf16)
    return call(merge_kernel, (shape, shape), 8, after=after, in_specs=[VM] * 4, out_specs=[VM] * 2)(
        pp, pm, above, below
    )


def settle_kernel(p0, a, b, keep, send):
    for out, start in ((send, ROWS), (keep, 0)):
        rows = slice(start, start + ROWS)
        total = p0[rows, :].astype(f32) + a[rows, :].astype(f32) + b[rows, :].astype(f32)
        out[...] = total.astype(bf16)


def settle(p0, a, b):
    shape = jax.ShapeDtypeStruct((ROWS, p0.shape[1]), bf16)
    return call(settle_kernel, (shape, shape), 8, in_specs=[VM] * 3, out_specs=[VM] * 2)(p0, a, b)


def finish_kernel(k0, k1, g0, g1, out, joined):
    c = lax.axis_index("row") % 2
    mine = pl.multiple_of(c * (3 * W), W)
    other = pl.multiple_of((1 - c) * (3 * W), W)
    for base, first, last in ((mine, k0, k1), (other, g0, g1)):
        joined[:, pl.ds(base, 2 * W)] = first[...]
        joined[:, pl.ds(pl.multiple_of(base + 2 * W, W), W)] = last[...]
    row = lax.broadcasted_iota(jnp.int32, (ROWS, ROWS), 0)
    col = lax.broadcasted_iota(jnp.int32, (ROWS, ROWS), 1)
    order = (col == row % BS * TROWS + row // BS).astype(f32).astype(bf16)
    out[...] = jnp.dot(order, joined[...], preferred_element_type=f32).astype(bf16)


def finish(kept, got):
    return call(
        finish_kernel,
        jax.ShapeDtypeStruct((ROWS, 6 * W), bf16),
        16,
        in_specs=[VM] * 4,
        out_specs=VM,
        scratch_shapes=[pltpu.VMEM((ROWS, 6 * W), bf16)],
    )(*kept, *got)


def body(
    orbitals,
    fock_blocks,
    fock_where,
    density_blocks,
    integrals,
    quartet_density,
    quartet_target,
    quartet_count,
):
    with jax.named_scope("fock"):
        fock = pack(fock_blocks, fock_where)
    with jax.named_scope("density"):
        ask_above = shift_row(quartet_density, -1)
        ask_below = shift_row(quartet_density, 1)
        pair = jnp.concatenate([density_blocks, swap_yh(density_blocks)], axis=0)
        moved0 = turned(orbitals, 0, (pair, ask_above, ask_below))
        pool = (pair, shift_z(pair, 1), shift_z(pair, -1), shift_z(pair, 2))
        own, for_above, for_below = select((quartet_density, ask_above, ask_below), pool)
        vectors = (own, shift_row(for_above, 1), shift_row(for_below, -1))
    with jax.named_scope("gather"):
        slots0 = join(*moved0, vectors[1:])
        left0, right0 = shift_x(slots0, 1), shift_x(slots0, -1)
        term = exchange(quartet_count, quartet_target, vectors, integrals)
        slots1 = join(*turned(orbitals, 1, (*vectors[1:], fock)), (term,))
        left1, right1 = shift_x(slots1, 1), shift_x(slots1, -1)
        far0, far1 = shift_x(left0, 1), shift_x(hold(right1, (left1,)), -1)
    with jax.named_scope("terms"):
        term = jnp.concatenate([term, swap_core(term)], axis=0)
        term = jnp.concatenate([term, swap_z(term, 1)], axis=0)
        term = hold(term, (slots1, left0, right0))
        term = jnp.concatenate([term, swap_yh(term)], axis=0)
    with jax.named_scope("fock"):
        fock_h = swap_yh(hold(fock, (term,)))
    with jax.named_scope("terms"):
        term = hold(term, (left1, right1))
        terms = (term, swap_z(term, 2))
    with jax.named_scope("fock"):
        near = tiles(True, (fock, swap_core(fock)), terms, ())
        fock_h = hold(fock_h, (near, far0, far1))
        far = tiles(False, (fock_h, swap_core(fock_h)), terms, ())
        mats = (near, far)
    with jax.named_scope("gather"):
        slots2 = join(*turned(orbitals, 2, terms[1:]), (far0, far1, far))
        left2, right2 = shift_x(slots2, 1), shift_x(slots2, -1)
    kept, got, mixed = [], [], ()
    for n in (2, 1):
        if n == 2:
            chunks = ((slots0, left0, right0, far0), (slots1, left1, right1, far1))
        else:
            with jax.named_scope("gather"):
                far2a = shift_x(hold(left2[:COLS], mixed), 1)
                far2b = shift_x(hold(right2[COLS:], mixed), -1)
            chunks = ((slots2, left2, right2, far2a, far2b),)
        with jax.named_scope("reduce"):
            (p2,) = product(mats, chunks, (2,), mixed)
            above, below = shift_z(p2[:ROWS], 1), shift_z(p2[ROWS:], -1)
            pp, pm = product(mats, chunks, (1, 3), tuple(kept), 20)
            pp, pm = merge(pp, pm, above, below, (left2, right2))
            mixed = (pp, pm)
            (p0,) = product(mats, chunks, (0,), mixed, 20)
            keep, send = settle(p0, shift_z(pp, 1), shift_z(pm, -1))
            kept.append(keep)
            got.append(swap_core(send))
    with jax.named_scope("finish"):
        return finish(kept, got)


def solution(mesh):
    return jax.shard_map(
        body,
        mesh=mesh,
        in_specs=(
            P("col", "row"),
            P(("row", "col"), None),
            P(("row", "col")),
            P(("row", "col"), None),
            P(("row", "col"), None, None),
            P(("row", "col")),
            P(("row", "col")),
            P(("row", "col")),
        ),
        out_specs=P("row", "col"),
        check_vma=False,
    )
```

profile of v0, /device:TPU:1, one launch (start us, length us, event | category | flops | bytes accessed | tf_op | source)
XLA Modules:
  0.0 165.6 jit_solution(11940916390559996526)
XLA Ops:
  0.0 1.4 collective-permute-start
  1.4 1.3 collective-permute-start.1
  2.8 2.7 %collective-permute-start.2 = (bf16[40,1024]{1,0:T(8,128)(2,1)}, bf16[40,1024]{1,0:T(8,128)(2,1)S(1)}, u32[]{:S(2)}, u32[]{:S(2)}) collective-permute-start(bf16[40,1024]{1,0:T(8,128)(2,1)} %param.11), channel_id=1, source_target_pairs={{0,1},{1,0},{2,3},{3,2},{4,5},{5,4},{6,7},{7,6},{8,9},{9,8},{10,11... | collective-permute-start | bytes 245768 | tf_op jit(solution)/shard_map/density/ppermute | solution.py:39
  5.5 0.9 constant_dynamic-update-slice_fusion.1
  6.4 1.3 collective-permute-done.2
  7.8 1.3 copy-done
  9.2 2.1 %collective-permute-start.8 = (bf16[1536,128]{1,0:T(8,128)(2,1)S(1)}, bf16[1536,128]{1,0:T(8,128)(2,1)S(1)}, u32[]{:S(2)}, u32[]{:S(2)}) collective-permute-start(bf16[1536,128]{1,0:T(8,128)(2,1)S(1)} %density.3), channel_id=1, source_target_pairs={{0,16},{1,0},{2,18},{3,2},{4,20},{5,4},{6,22},{7,6},{8,24},{9,8},{... | collective-permute-start | bytes 1179656 | tf_op jit(solution)/shard_map/density/ppermute | solution.py:39
  11.3 0.7 collective-permute-start.9
  11.9 1.7 %collective-permute-start.3 = (bf16[80,1024]{1,0:T(8,128)(2,1)S(1)}, bf16[80,1024]{1,0:T(8,128)(2,1)S(1)}, u32[]{:S(2)}, u32[]{:S(2)}) collective-permute-start(bf16[80,1024]{1,0:T(8,128)(2,1)S(1)} %constant_dynamic-update-slice_fusion.refs_3_.refs_0_), channel_id=1, source_target_pairs={{0,2},{1,3},{2,4},{3,5},{4,6},{5,7},{6,0},{7,1},{8,10},{9,11},{10,... | collective-permute-start | bytes 491528 | tf_op jit(solution)/shard_map/density/ppermute | solution.py:39
  13.6 2.2 %collective-permute-start.4 = (bf16[80,1024]{1,0:T(8,128)(2,1)S(1)}, bf16[80,1024]{1,0:T(8,128)(2,1)S(1)}, u32[]{:S(2)}, u32[]{:S(2)}) collective-permute-start(bf16[80,1024]{1,0:T(8,128)(2,1)S(1)} %constant_dynamic-update-slice_fusion.refs_3_.refs_0_), channel_id=1, source_target_pairs={{0,6},{1,7},{2,0},{3,1},{4,2},{5,3},{6,4},{7,5},{8,14},{9,15},{10,... | collective-permute-start | bytes 491528 | tf_op jit(solution)/shard_map/density/ppermute | solution.py:39
  15.8 1.2 collective-permute-start.5
  17.1 2.0 %collective-permute-done.3.refs_4_ = bf16[80,1024]{1,0:T(8,128)(2,1)S(1)} collective-permute-done((bf16[80,1024]{1,0:T(8,128)(2,1)S(1)}, bf16[80,1024]{1,0:T(8,128)(2,1)S(1)}, u32[]{:S(2)}, u32[]{:S(2)}) %collective-permute-start.3) | collective-permute-done | bytes 163872 | tf_op jit(solution)/shard_map/density/ppermute | solution.py:39
  19.0 4.5 %collective-permute-done.5.refs_6_ = bf16[80,1024]{1,0:T(8,128)(2,1)S(1)} collective-permute-done((bf16[80,1024]{1,0:T(8,128)(2,1)S(1)}, bf16[80,1024]{1,0:T(8,128)(2,1)S(1)}, u32[]{:S(2)}, u32[]{:S(2)}) %collective-permute-start.5) | collective-permute-done | bytes 163872 | tf_op jit(solution)/shard_map/density/ppermute | solution.py:39
  23.6 0.9 density.2
  24.5 5.3 %collective-permute-start.6 = (bf16[16,1024]{1,0:T(8,128)(2,1)S(1)}, bf16[16,1024]{1,0:T(8,128)(2,1)S(1)}, u32[]{:S(2)}, u32[]{:S(2)}) collective-permute-start(bf16[16,1024]{1,0:T(8,128)(2,1)S(1)} %get-tuple-element.20), channel_id=1, source_target_pairs={{0,8},{1,9},{2,10},{3,11},{4,12},{5,13},{6,14},{7,15},{8,16},{9,17... | collective-permute-start | bytes 98312 | tf_op jit(solution)/shard_map/density/ppermute | solution.py:64
  29.8 1.0 collective-permute-done.6.refs_0_.refs_3_
  30.8 2.6 %collective-permute-done.7.refs_1_.refs_4_ = bf16[16,1024]{1,0:T(8,128)(2,1)S(1)} collective-permute-done((bf16[16,1024]{1,0:T(8,128)(2,1)S(1)}, bf16[16,1024]{1,0:T(8,128)(2,1)S(1)}, u32[]{:S(2)}, u32[]{:S(2)}) %collective-permute-start.7) | collective-permute-done | bytes 32800 | tf_op jit(solution)/shard_map/density/ppermute | solution.py:64
  33.9 0.9 collective-permute-start.10
  34.7 2.5 %collective-permute-start.18 = (bf16[3072,128]{1,0:T(8,128)(2,1)S(1)}, bf16[3072,128]{1,0:T(8,128)(2,1)S(1)}, u32[]{:S(2)}, u32[]{:S(2)}) collective-permute-start(bf16[3072,128]{1,0:T(8,128)(2,1)S(1)} %gather.9.refs_2_.refs_4_), channel_id=1, source_target_pairs={{0,96},{1,97},{2,98},{3,99},{4,100},{5,101},{6,102},{7,103},{8,104... | collective-permute-start | bytes 2359304 | tf_op jit(solution)/shard_map/gather/ppermute | solution.py:39
  37.5 2.0 %collective-permute-start.12 = (bf16[1536,128]{1,0:T(8,128)(2,1)S(1)}, bf16[1536,128]{1,0:T(8,128)(2,1)S(1)}, u32[]{:S(2)}, u32[]{:S(2)}) collective-permute-start(bf16[1536,128]{1,0:T(8,128)(2,1)S(1)} %gather.11), channel_id=1, source_target_pairs={{0,16},{1,0},{2,18},{3,2},{4,20},{5,4},{6,22},{7,6},{8,24},{9,8},{... | collective-permute-start | bytes 1179656 | tf_op jit(solution)/shard_map/gather/ppermute | solution.py:39
  39.4 0.7 collective-permute-start.13
  40.8 7.0 %gather.10.refs_0_ = bf16[8,1152]{1,0:T(8,128)(2,1)S(1)} custom-call(s32[1]{0:T(128)S(6)} %copy.10.refs_0_, s32[8]{0:T(128)S(1)} %copy-done.4, bf16[16,1024]{1,0:T(8,128)(2,1)S(1)} %get-tuple-element.22.refs_2_, bf16[16,1024]{1,0:T(8,128)(2,1)S(1)} %collective-permute-done.6.refs_0_.refs_3_, bf16[16,1024]{1,0:T(8,128)(2,1)S(1)} %collective-permute-done.7.refs_1_.refs_4_, ...), custom_call_target="tpu_custom_call" | custom-call | flops 1 | bytes 1 | tf_op jit(solution)/shard_map/gather/pallas_call | solution.py:90
  47.8 1.2 collective-permute-done.19
  49.0 0.6 collective-permute-start.20
  50.1 2.7 %collective-permute-start.15 = (bf16[3072,128]{1,0:T(8,128)(2,1)S(1)}, bf16[3072,128]{1,0:T(8,128)(2,1)S(1)}, u32[]{:S(2)}, u32[]{:S(2)}) collective-permute-start(bf16[3072,128]{1,0:T(8,128)(2,1)S(1)} %gather.12.refs_0_.refs_6_.refs_8_), channel_id=1, source_target_pairs={{0,96},{1,97},{2,98},{3,99},{4,100},{5,101},{6,102},{7,103},{8,104... | collective-permute-start | bytes 2359304 | tf_op jit(solution)/shard_map/gather/ppermute | solution.py:39
  52.8 1.1 collective-permute-done.10.refs_1_.refs_3_.refs_5_
  54.0 3.8 %collective-permute-start.21 = (bf16[32,1152]{1,0:T(8,128)(2,1)S(1)}, bf16[32,1152]{1,0:T(8,128)(2,1)S(1)}, u32[]{:S(2)}, u32[]{:S(2)}) collective-permute-start(bf16[32,1152]{1,0:T(8,128)(2,1)S(1)} %terms.2), channel_id=1, source_target_pairs={{0,1},{1,0},{2,3},{3,2},{4,5},{5,4},{6,7},{7,6},{8,9},{9,8},{10,11... | collective-permute-start | bytes 221192 | tf_op jit(solution)/shard_map/terms/ppermute | solution.py:39
  57.8 1.3 collective-permute-start.17
  59.7 3.3 %collective-permute-start.23 = (bf16[528,1024]{1,0:T(8,128)(2,1)S(1)}, bf16[528,1024]{1,0:T(8,128)(2,1)S(1)}, u32[]{:S(2)}, u32[]{:S(2)}) collective-permute-start(bf16[528,1024]{1,0:T(8,128)(2,1)S(1)} %fock.7), channel_id=1, source_target_pairs={{0,1},{1,0},{2,3},{3,2},{4,5},{5,4},{6,7},{7,6},{8,9},{9,8},{10,11... | collective-permute-start | bytes 3244040 | tf_op jit(solution)/shard_map/fock/ppermute | solution.py:39
  63.1 7.9 %collective-permute-done.14.refs_0_.refs_7_.refs_9_ = bf16[3072,128]{1,0:T(8,128)(2,1)S(1)} collective-permute-done((bf16[3072,128]{1,0:T(8,128)(2,1)S(1)}, bf16[3072,128]{1,0:T(8,128)(2,1)S(1)}, u32[]{:S(2)}, u32[]{:S(2)}) %collective-permute-start.14) | collective-permute-done | bytes 786464 | tf_op jit(solution)/shard_map/gather/ppermute | solution.py:39
  71.0 2.7 %collective-permute-start.16 = (bf16[3072,128]{1,0:T(8,128)(2,1)S(1)}, bf16[3072,128]{1,0:T(8,128)(2,1)S(1)}, u32[]{:S(2)}, u32[]{:S(2)}) collective-permute-start(bf16[3072,128]{1,0:T(8,128)(2,1)S(1)} %gather.13), channel_id=1, source_target_pairs={{0,96},{1,97},{2,98},{3,99},{4,100},{5,101},{6,102},{7,103},{8,104... | collective-permute-start | bytes 2359304 | tf_op jit(solution)/shard_map/gather/ppermute | solution.py:39
  73.9 1.1 collective-permute-start.22
  75.1 4.9 %collective-permute-done.22.refs_3_.refs_0_ = bf16[64,1152]{1,0:T(8,128)(2,1)S(1)} collective-permute-done((bf16[64,1152]{1,0:T(8,128)(2,1)S(1)}, bf16[64,1152]{1,0:T(8,128)(2,1)S(1)}, u32[]{:S(2)}, u32[]{:S(2)}) %collective-permute-start.22) | collective-permute-done | bytes 147488 | tf_op jit(solution)/shard_map/terms/ppermute | solution.py:39
  80.0 6.5 %fock.6.refs_0_.refs_2_.refs_1_ = bf16[1536,1536]{1,0:T(8,128)(2,1)S(1)} custom-call(bf16[528,1024]{1,0:T(8,128)(2,1)S(1)} %fock.5.refs_2_.refs_0_.refs_1_, bf16[528,1024]{1,0:T(8,128)(2,1)S(1)} %collective-permute-done.17.refs_1_, bf16[64,1152]{1,0:T(8,128)(2,1)S(1)} %terms.3.refs_2_, bf16[64,1152]{1,0:T(8,128)(2,1)S(1)} %collective-permute-done.22.refs_3_.refs_0_), custom_call_target="tpu_custom_call" | custom-call | flops 1 | bytes 1 | tf_op jit(solution)/shard_map/fock/pallas_call | solution.py:90
  86.5 1.3 collective-permute-done.11.refs_1_.refs_0_.refs_5_.refs_7_
  87.8 1.1 collective-permute-done.16.refs_2_.refs_1_.refs_9_.refs_11_
  89.1 2.7 %collective-permute-start.24 = (bf16[528,1024]{1,0:T(8,128)(2,1)S(1)}, bf16[528,1024]{1,0:T(8,128)(2,1)S(1)}, u32[]{:S(2)}, u32[]{:S(2)}) collective-permute-start(bf16[528,1024]{1,0:T(8,128)(2,1)S(1)} %fock.8.refs_0_), channel_id=1, source_target_pairs={{0,8},{1,9},{2,10},{3,11},{4,12},{5,13},{6,14},{7,15},{8,0},{9,1},... | collective-permute-start | bytes 3244040 | tf_op jit(solution)/shard_map/fock/ppermute | solution.py:39
  91.8 2.9 %collective-permute-start.25 = (bf16[1536,128]{1,0:T(8,128)(2,1)S(1)}, bf16[1536,128]{1,0:T(8,128)(2,1)S(1)}, u32[]{:S(2)}, u32[]{:S(2)}) collective-permute-start(bf16[1536,128]{1,0:T(8,128)(2,1)S(1)} %gather.14), channel_id=1, source_target_pairs={{0,16},{1,0},{2,18},{3,2},{4,20},{5,4},{6,22},{7,6},{8,24},{9,8},{... | collective-permute-start | bytes 1179656 | tf_op jit(solution)/shard_map/gather/ppermute | solution.py:39
  94.7 0.7 collective-permute-start.26
  95.4 6.5 %fock.9.refs_2_.refs_1_.refs_3_ = bf16[1536,1536]{1,0:T(8,128)(2,1)S(1)} custom-call(bf16[528,1024]{1,0:T(8,128)(2,1)S(1)} %fock.8.refs_0_, bf16[528,1024]{1,0:T(8,128)(2,1)S(1)} %collective-permute-done.24.refs_1_, bf16[64,1152]{1,0:T(8,128)(2,1)S(1)} %terms.3.refs_2_, bf16[64,1152]{1,0:T(8,128)(2,1)S(1)} %collective-permute-done.22.refs_3_.refs_0_), custom_call_target="tpu_custom_call" | custom-call | flops 1 | bytes 1 | tf_op jit(solution)/shard_map/fock/pallas_call | solution.py:90
  102.0 3.0 %collective-permute-done.25.refs_3_ = bf16[1536,128]{1,0:T(8,128)(2,1)S(1)} collective-permute-done((bf16[1536,128]{1,0:T(8,128)(2,1)S(1)}, bf16[1536,128]{1,0:T(8,128)(2,1)S(1)}, u32[]{:S(2)}, u32[]{:S(2)}) %collective-permute-start.25) | collective-permute-done | bytes 393248 | tf_op jit(solution)/shard_map/gather/ppermute | solution.py:39
  105.3 0.7 collective-permute-start.27
  106.0 2.9 %collective-permute-start.28 = (bf16[3072,128]{1,0:T(8,128)(2,1)S(1)}, bf16[3072,128]{1,0:T(8,128)(2,1)S(1)}, u32[]{:S(2)}, u32[]{:S(2)}) collective-permute-start(bf16[3072,128]{1,0:T(8,128)(2,1)S(1)} %gather.15.refs_3_.refs_4_), channel_id=1, source_target_pairs={{0,96},{1,97},{2,98},{3,99},{4,100},{5,101},{6,102},{7,103},{8,104... | collective-permute-start | bytes 2359304 | tf_op jit(solution)/shard_map/gather/ppermute | solution.py:39
  108.9 3.0 %reduce.11 = bf16[1536,256]{1,0:T(8,128)(2,1)S(1)} custom-call(bf16[1536,1536]{1,0:T(8,128)(2,1)S(1)} %fock.6.refs_0_.refs_2_.refs_1_, bf16[1536,1536]{1,0:T(8,128)(2,1)S(1)} %fock.9.refs_2_.refs_1_.refs_3_, bf16[3072,128]{1,0:T(8,128)(2,1)S(1)} %gather.9.refs_2_.refs_4_, bf16[3072,128]{1,0:T(8,128)(2,1)S(1)} %collective-permute-done.10.refs_1_.refs_3_.refs_5_, ...), custom_call_target="tpu_custom_call" | custom-call | flops 1 | bytes 1 | tf_op jit(solution)/shard_map/reduce/pallas_call | solution.py:90
  112.0 0.5 collective-permute-start.29
  112.5 2.3 %collective-permute-start.30 = (bf16[768,256]{1,0:T(8,128)(2,1)S(1)}, bf16[768,256]{1,0:T(8,128)(2,1)S(1)}, u32[]{:S(2)}, u32[]{:S(2)}) collective-permute-start(bf16[768,256]{1,0:T(8,128)(2,1)S(1)} %get-tuple-element.35), channel_id=1, source_target_pairs={{0,6},{1,7},{2,0},{3,1},{4,2},{5,3},{6,4},{7,5},{8,14},{9,15},{10,... | collective-permute-start | bytes 1179656 | tf_op jit(solution)/shard_map/reduce/ppermute | solution.py:39
  114.7 6.0 %reduce.10 = (bf16[1536,256]{1,0:T(8,128)(2,1)S(1)}, bf16[1536,256]{1,0:T(8,128)(2,1)S(1)}) custom-call(bf16[1536,1536]{1,0:T(8,128)(2,1)S(1)} %fock.6.refs_0_.refs_2_.refs_1_, bf16[1536,1536]{1,0:T(8,128)(2,1)S(1)} %fock.9.refs_2_.refs_1_.refs_3_, bf16[3072,128]{1,0:T(8,128)(2,1)S(1)} %gather.9.refs_2_.refs_4_, ...), custom_call_target="tpu_custom_call" | custom-call | flops 20000000000 | bytes 1 | tf_op jit(solution)/shard_map/reduce/pallas_call | solution.py:90
  120.7 2.3 %collective-permute-done.29.refs_4_ = bf16[768,256]{1,0:T(8,128)(2,1)S(1)} collective-permute-done((bf16[768,256]{1,0:T(8,128)(2,1)S(1)}, bf16[768,256]{1,0:T(8,128)(2,1)S(1)}, u32[]{:S(2)}, u32[]{:S(2)}) %collective-permute-start.29) | collective-permute-done | bytes 393248 | tf_op jit(solution)/shard_map/reduce/ppermute | solution.py:39
  123.0 3.1 %collective-permute-done.27.refs_0_.refs_4_.refs_5_ = bf16[3072,128]{1,0:T(8,128)(2,1)S(1)} collective-permute-done((bf16[3072,128]{1,0:T(8,128)(2,1)S(1)}, bf16[3072,128]{1,0:T(8,128)(2,1)S(1)}, u32[]{:S(2)}, u32[]{:S(2)}) %collective-permute-start.27) | collective-permute-done | bytes 786464 | tf_op jit(solution)/shard_map/gather/ppermute | solution.py:39
  126.8 2.5 %collective-permute-start.32 = (bf16[1536,256]{1,0:T(8,128)(2,1)S(1)}, bf16[1536,256]{1,0:T(8,128)(2,1)S(1)}, u32[]{:S(2)}, u32[]{:S(2)}) collective-permute-start(bf16[1536,256]{1,0:T(8,128)(2,1)S(1)} %get-tuple-element.26.refs_1_), channel_id=1, source_target_pairs={{0,6},{1,7},{2,0},{3,1},{4,2},{5,3},{6,4},{7,5},{8,14},{9,15},{10,... | collective-permute-start | bytes 2359304 | tf_op jit(solution)/shard_map/reduce/ppermute | solution.py:39
  129.5 0.6 collective-permute-start.33
  130.3 2.2 %collective-permute-start.34 = (bf16[1536,128]{1,0:T(8,128)(2,1)S(1)}, bf16[1536,128]{1,0:T(8,128)(2,1)S(1)}, u32[]{:S(2)}, u32[]{:S(2)}) collective-permute-start(bf16[1536,128]{1,0:T(8,128)(2,1)S(1)} %gather.17), channel_id=1, source_target_pairs={{0,96},{1,97},{2,98},{3,99},{4,100},{5,101},{6,102},{7,103},{8,104... | collective-permute-start | bytes 1179656 | tf_op jit(solution)/shard_map/gather/ppermute | solution.py:39
  132.5 3.0 %reduce.13.refs_0_ = bf16[1536,256]{1,0:T(8,128)(2,1)S(1)} custom-call(bf16[1536,256]{1,0:T(8,128)(2,1)S(1)} %get-tuple-element.25.refs_0_, bf16[1536,256]{1,0:T(8,128)(2,1)S(1)} %get-tuple-element.26.refs_1_, bf16[1536,1536]{1,0:T(8,128)(2,1)S(1)} %fock.6.refs_0_.refs_2_.refs_1_, bf16[1536,1536]{1,0:T(8,128)(2,1)S(1)} %fock.9.refs_2_.refs_1_.refs_3_, ...), custom_call_target="tpu_custom_call" | custom-call | flops 20000000000 | bytes 1 | tf_op jit(solution)/shard_map/reduce/pallas_call | solution.py:90
  135.5 4.1 %collective-permute-done.33.refs_6_.refs_7_ = bf16[1536,128]{1,0:T(8,128)(2,1)S(1)} collective-permute-done((bf16[1536,128]{1,0:T(8,128)(2,1)S(1)}, bf16[1536,128]{1,0:T(8,128)(2,1)S(1)}, u32[]{:S(2)}, u32[]{:S(2)}) %collective-permute-start.33) | collective-permute-done | bytes 393248 | tf_op jit(solution)/shard_map/gather/ppermute | solution.py:39
  139.7 3.0 %reduce.16 = bf16[1536,128]{1,0:T(8,128)(2,1)S(1)} custom-call(bf16[1536,256]{1,0:T(8,128)(2,1)S(1)} %get-tuple-element.25.refs_0_, bf16[1536,256]{1,0:T(8,128)(2,1)S(1)} %get-tuple-element.26.refs_1_, bf16[1536,1536]{1,0:T(8,128)(2,1)S(1)} %fock.6.refs_0_.refs_2_.refs_1_, bf16[1536,1536]{1,0:T(8,128)(2,1)S(1)} %fock.9.refs_2_.refs_1_.refs_3_, ...), custom_call_target="tpu_custom_call" | custom-call | flops 1 | bytes 1 | tf_op jit(solution)/shard_map/reduce/pallas_call | solution.py:90
  142.8 2.7 %collective-permute-start.36 = (bf16[768,128]{1,0:T(8,128)(2,1)S(1)}, bf16[768,128]{1,0:T(8,128)(2,1)S(1)}, u32[]{:S(2)}, u32[]{:S(2)}) collective-permute-start(bf16[768,128]{1,0:T(8,128)(2,1)S(1)} %get-tuple-element.37), channel_id=1, source_target_pairs={{0,6},{1,7},{2,0},{3,1},{4,2},{5,3},{6,4},{7,5},{8,14},{9,15},{10,... | collective-permute-start | bytes 589832 | tf_op jit(solution)/shard_map/reduce/ppermute | solution.py:39
  145.9 3.0 %reduce.15 = (bf16[1536,128]{1,0:T(8,128)(2,1)S(1)}, bf16[1536,128]{1,0:T(8,128)(2,1)S(1)}) custom-call(bf16[768,256]{1,0:T(8,128)(2,1)S(1)} %get-tuple-element.27.refs_0_, bf16[1536,1536]{1,0:T(8,128)(2,1)S(1)} %fock.6.refs_0_.refs_2_.refs_1_, bf16[1536,1536]{1,0:T(8,128)(2,1)S(1)} %fock.9.refs_2_.refs_1_.refs_3_, ...), custom_call_target="tpu_custom_call" | custom-call | flops 20000000000 | bytes 1 | tf_op jit(solution)/shard_map/reduce/pallas_call | solution.py:90
  149.1 1.2 collective-permute-start.37
  150.4 1.7 %collective-permute-start.38 = (bf16[1536,128]{1,0:T(8,128)(2,1)S(1)}, bf16[1536,128]{1,0:T(8,128)(2,1)S(1)}, u32[]{:S(2)}, u32[]{:S(2)}) collective-permute-start(bf16[1536,128]{1,0:T(8,128)(2,1)S(1)} %get-tuple-element.31.refs_1_), channel_id=1, source_target_pairs={{0,6},{1,7},{2,0},{3,1},{4,2},{5,3},{6,4},{7,5},{8,14},{9,15},{10,... | collective-permute-start | bytes 1179656 | tf_op jit(solution)/shard_map/reduce/ppermute | solution.py:39
  152.1 3.7 %collective-permute-start.39 = (bf16[768,256]{1,0:T(8,128)(2,1)S(1)}, bf16[768,256]{1,0:T(8,128)(2,1)S(1)}, u32[]{:S(2)}, u32[]{:S(2)}) collective-permute-start(bf16[768,256]{1,0:T(8,128)(2,1)S(1)} %get-tuple-element.33), channel_id=1, source_target_pairs={{0,8},{1,9},{2,10},{3,11},{4,12},{5,13},{6,14},{7,15},{8,0},{9,1},... | collective-permute-start | bytes 1179656 | tf_op jit(solution)/shard_map/reduce/ppermute | solution.py:39
  155.8 3.3 %reduce.18.refs_0_ = bf16[1536,128]{1,0:T(8,128)(2,1)S(1)} custom-call(bf16[1536,128]{1,0:T(8,128)(2,1)S(1)} %get-tuple-element.30.refs_0_, bf16[1536,128]{1,0:T(8,128)(2,1)S(1)} %get-tuple-element.31.refs_1_, bf16[1536,1536]{1,0:T(8,128)(2,1)S(1)} %fock.6.refs_0_.refs_2_.refs_1_, bf16[1536,1536]{1,0:T(8,128)(2,1)S(1)} %fock.9.refs_2_.refs_1_.refs_3_, ...), custom_call_target="tpu_custom_call" | custom-call | flops 20000000000 | bytes 1 | tf_op jit(solution)/shard_map/reduce/pallas_call | solution.py:90
  159.3 3.0 %collective-permute-start.40 = (bf16[768,128]{1,0:T(8,128)(2,1)S(1)}, bf16[768,128]{1,0:T(8,128)(2,1)S(1)}, u32[]{:S(2)}, u32[]{:S(2)}) collective-permute-start(bf16[768,128]{1,0:T(8,128)(2,1)S(1)} %get-tuple-element.34), channel_id=1, source_target_pairs={{0,8},{1,9},{2,10},{3,11},{4,12},{5,13},{6,14},{7,15},{8,0},{9,1},... | collective-permute-start | bytes 589832 | tf_op jit(solution)/shard_map/reduce/ppermute | solution.py:39
  162.3 1.1 collective-permute-done.40.refs_3_
  163.4 2.3 %finish.1 = bf16[768,768]{1,0:T(8,128)(2,1)} custom-call(bf16[768,256]{1,0:T(8,128)(2,1)S(1)} %get-tuple-element.27.refs_0_, bf16[768,128]{1,0:T(8,128)(2,1)S(1)} %get-tuple-element.32.refs_1_, bf16[768,256]{1,0:T(8,128)(2,1)S(1)} %collective-permute-done.39.refs_2_, bf16[768,128]{1,0:T(8,128)(2,1)S(1)} %collective-permute-done.40.refs_3_), custom_call_target="tpu_custom_call" | custom-call | flops 1 | bytes 1 | tf_op jit(solution)/shard_map/finish/pallas_call | solution.py:90
  (68 shorter events, 4.7 us)
Async XLA Ops:
  0.0 23.6 %copy-start.5 = (s32[8]{0:T(128)S(1)}, s32[8]{0:T(128)}, u32[]{:S(2)}) copy-start(s32[8]{0:T(128)} %refs_0_.3) | copy-start | bytes 100
  0.0 7.8 %collective-permute-start = (s32[8]{0:T(128)}, s32[8]{0:T(128)S(1)}, u32[]{:S(2)}, u32[]{:S(2)}) collective-permute-start(s32[8]{0:T(128)} %refs_0_.3), channel_id=1, source_target_pairs={{0,120},{1,121},{2,122},{3,123},{4,124},{5,125},{6,126},{7,127},{8... | collective-permute-start | bytes 104 | tf_op jit(solution)/shard_map/density/ppermute | solution.py:64
  1.4 6.4 %collective-permute-start.1 = (s32[8]{0:T(128)}, s32[8]{0:T(128)S(1)}, u32[]{:S(2)}, u32[]{:S(2)}) collective-permute-start(s32[8]{0:T(128)} %refs_0_.3), channel_id=1, source_target_pairs={{0,8},{1,9},{2,10},{3,11},{4,12},{5,13},{6,14},{7,15},{8,16},{9,17... | collective-permute-start | bytes 104 | tf_op jit(solution)/shard_map/density/ppermute | solution.py:64
  2.8 5.0 %collective-permute-start.2 = (bf16[40,1024]{1,0:T(8,128)(2,1)}, bf16[40,1024]{1,0:T(8,128)(2,1)S(1)}, u32[]{:S(2)}, u32[]{:S(2)}) collective-permute-start(bf16[40,1024]{1,0:T(8,128)(2,1)} %param.11), channel_id=1, source_target_pairs={{0,1},{1,0},{2,3},{3,2},{4,5},{5,4},{6,7},{7,6},{8,9},{9,8},{10,11... | collective-permute-start | bytes 245768 | tf_op jit(solution)/shard_map/density/ppermute | solution.py:39
  7.8 1.3 copy-start
  9.2 28.1 %copy-start.2 = (bf16[512,1024]{1,0:T(8,128)(2,1)S(1)}, bf16[512,1024]{1,0:T(8,128)(2,1)}, u32[]{:S(2)}) copy-start(bf16[512,1024]{1,0:T(8,128)(2,1)} %refs_0_.4) | copy-start | bytes 3145732
  9.2 28.1 %copy-start.3 = (s32[512]{0:T(512)S(1)}, s32[512]{0:T(512)}, u32[]{:S(2)}) copy-start(s32[512]{0:T(512)} %param.10) | copy-start | bytes 6148
  9.2 24.3 %collective-permute-start.8 = (bf16[1536,128]{1,0:T(8,128)(2,1)S(1)}, bf16[1536,128]{1,0:T(8,128)(2,1)S(1)}, u32[]{:S(2)}, u32[]{:S(2)}) collective-permute-start(bf16[1536,128]{1,0:T(8,128)(2,1)S(1)} %density.3), channel_id=1, source_target_pairs={{0,16},{1,0},{2,18},{3,2},{4,20},{5,4},{6,22},{7,6},{8,24},{9,8},{... | collective-permute-start | bytes 1179656 | tf_op jit(solution)/shard_map/density/ppermute | solution.py:39
  11.3 22.2 %collective-permute-start.9 = (bf16[1536,128]{1,0:T(8,128)(2,1)S(1)}, bf16[1536,128]{1,0:T(8,128)(2,1)S(1)}, u32[]{:S(2)}, u32[]{:S(2)}) collective-permute-start(bf16[1536,128]{1,0:T(8,128)(2,1)S(1)} %density.3), channel_id=1, source_target_pairs={{0,0},{1,16},{2,2},{3,18},{4,4},{5,20},{6,6},{7,22},{8,8},{9,24},{... | collective-permute-start | bytes 1179656 | tf_op jit(solution)/shard_map/density/ppermute | solution.py:39
  11.9 7.1 %collective-permute-start.3 = (bf16[80,1024]{1,0:T(8,128)(2,1)S(1)}, bf16[80,1024]{1,0:T(8,128)(2,1)S(1)}, u32[]{:S(2)}, u32[]{:S(2)}) collective-permute-start(bf16[80,1024]{1,0:T(8,128)(2,1)S(1)} %constant_dynamic-update-slice_fusion.refs_3_.refs_0_), channel_id=1, source_target_pairs={{0,2},{1,3},{2,4},{3,5},{4,6},{5,7},{6,0},{7,1},{8,10},{9,11},{10,... | collective-permute-start | bytes 491528 | tf_op jit(solution)/shard_map/density/ppermute | solution.py:39
  13.6 5.4 %collective-permute-start.4 = (bf16[80,1024]{1,0:T(8,128)(2,1)S(1)}, bf16[80,1024]{1,0:T(8,128)(2,1)S(1)}, u32[]{:S(2)}, u32[]{:S(2)}) collective-permute-start(bf16[80,1024]{1,0:T(8,128)(2,1)S(1)} %constant_dynamic-update-slice_fusion.refs_3_.refs_0_), channel_id=1, source_target_pairs={{0,6},{1,7},{2,0},{3,1},{4,2},{5,3},{6,4},{7,5},{8,14},{9,15},{10,... | collective-permute-start | bytes 491528 | tf_op jit(solution)/shard_map/density/ppermute | solution.py:39
  15.8 7.7 %collective-permute-start.5 = (bf16[80,1024]{1,0:T(8,128)(2,1)S(1)}, bf16[80,1024]{1,0:T(8,128)(2,1)S(1)}, u32[]{:S(2)}, u32[]{:S(2)}) collective-permute-start(bf16[80,1024]{1,0:T(8,128)(2,1)S(1)} %constant_dynamic-update-slice_fusion.refs_3_.refs_0_), channel_id=1, source_target_pairs={{0,4},{1,5},{2,6},{3,7},{4,0},{5,1},{6,2},{7,3},{8,12},{9,13},{10,... | collective-permute-start | bytes 491528 | tf_op jit(solution)/shard_map/density/ppermute | solution.py:39
  24.5 6.3 %collective-permute-start.6 = (bf16[16,1024]{1,0:T(8,128)(2,1)S(1)}, bf16[16,1024]{1,0:T(8,128)(2,1)S(1)}, u32[]{:S(2)}, u32[]{:S(2)}) collective-permute-start(bf16[16,1024]{1,0:T(8,128)(2,1)S(1)} %get-tuple-element.20), channel_id=1, source_target_pairs={{0,8},{1,9},{2,10},{3,11},{4,12},{5,13},{6,14},{7,15},{8,16},{9,17... | collective-permute-start | bytes 98312 | tf_op jit(solution)/shard_map/density/ppermute | solution.py:64
  29.8 3.6 %collective-permute-start.7 = (bf16[16,1024]{1,0:T(8,128)(2,1)S(1)}, bf16[16,1024]{1,0:T(8,128)(2,1)S(1)}, u32[]{:S(2)}, u32[]{:S(2)}) collective-permute-start(bf16[16,1024]{1,0:T(8,128)(2,1)S(1)} %get-tuple-element.21), channel_id=1, source_target_pairs={{0,120},{1,121},{2,122},{3,123},{4,124},{5,125},{6,126},{7,127},{8... | collective-permute-start | bytes 98312 | tf_op jit(solution)/shard_map/density/ppermute | solution.py:64
  33.8 3.5 %copy-start.1 = (bf16[1536,384]{1,0:T(8,128)(2,1)S(1)}, bf16[1536,384]{1,0:T(8,128)(2,1)}, u32[]{:S(2)}) copy-start(bf16[1536,384]{1,0:T(8,128)(2,1)} %refs_1_.3) | copy-start | bytes 3538948
  33.9 20.1 %collective-permute-start.10 = (bf16[3072,128]{1,0:T(8,128)(2,1)S(1)}, bf16[3072,128]{1,0:T(8,128)(2,1)S(1)}, u32[]{:S(2)}, u32[]{:S(2)}) collective-permute-start(bf16[3072,128]{1,0:T(8,128)(2,1)S(1)} %gather.9.refs_2_.refs_4_), channel_id=1, source_target_pairs={{0,32},{1,33},{2,34},{3,35},{4,36},{5,37},{6,38},{7,39},{8,40},{9,... | collective-permute-start | bytes 2359304 | tf_op jit(solution)/shard_map/gather/ppermute | solution.py:39
  34.7 19.2 %collective-permute-start.18 = (bf16[3072,128]{1,0:T(8,128)(2,1)S(1)}, bf16[3072,128]{1,0:T(8,128)(2,1)S(1)}, u32[]{:S(2)}, u32[]{:S(2)}) collective-permute-start(bf16[3072,128]{1,0:T(8,128)(2,1)S(1)} %gather.9.refs_2_.refs_4_), channel_id=1, source_target_pairs={{0,96},{1,97},{2,98},{3,99},{4,100},{5,101},{6,102},{7,103},{8,104... | collective-permute-start | bytes 2359304 | tf_op jit(solution)/shard_map/gather/ppermute | solution.py:39
  37.4 3.4 %copy-start.4 = (s32[8]{0:T(128)S(1)}, s32[8]{0:T(128)}, u32[]{:S(2)}) copy-start(s32[8]{0:T(128)} %refs_1_.2) | copy-start | bytes 100
  37.5 12.2 %collective-permute-start.12 = (bf16[1536,128]{1,0:T(8,128)(2,1)S(1)}, bf16[1536,128]{1,0:T(8,128)(2,1)S(1)}, u32[]{:S(2)}, u32[]{:S(2)}) collective-permute-start(bf16[1536,128]{1,0:T(8,128)(2,1)S(1)} %gather.11), channel_id=1, source_target_pairs={{0,16},{1,0},{2,18},{3,2},{4,20},{5,4},{6,22},{7,6},{8,24},{9,8},{... | collective-permute-start | bytes 1179656 | tf_op jit(solution)/shard_map/gather/ppermute | solution.py:39
  39.4 10.2 %collective-permute-start.13 = (bf16[1536,128]{1,0:T(8,128)(2,1)S(1)}, bf16[1536,128]{1,0:T(8,128)(2,1)S(1)}, u32[]{:S(2)}, u32[]{:S(2)}) collective-permute-start(bf16[1536,128]{1,0:T(8,128)(2,1)S(1)} %gather.11), channel_id=1, source_target_pairs={{0,0},{1,16},{2,2},{3,18},{4,4},{5,20},{6,6},{7,22},{8,8},{9,24},{... | collective-permute-start | bytes 1179656 | tf_op jit(solution)/shard_map/gather/ppermute | solution.py:39
  47.7 1.3 collective-permute-start.19
  49.0 3.8 %collective-permute-start.20 = (bf16[16,1152]{1,0:T(8,128)(2,1)S(1)}, bf16[16,1152]{1,0:T(8,128)(2,1)S(1)}, u32[]{:S(2)}, u32[]{:S(2)}) collective-permute-start(bf16[16,1152]{1,0:T(8,128)(2,1)S(1)} %pad_maximum_fusion.2), channel_id=1, source_target_pairs={{0,2},{1,3},{2,0},{3,1},{4,6},{5,7},{6,4},{7,5},{8,10},{9,11},{10,... | collective-permute-start | bytes 110600 | tf_op jit(solution)/shard_map/terms/ppermute | solution.py:39
  50.0 20.9 %collective-permute-start.14 = (bf16[3072,128]{1,0:T(8,128)(2,1)S(1)}, bf16[3072,128]{1,0:T(8,128)(2,1)S(1)}, u32[]{:S(2)}, u32[]{:S(2)}) collective-permute-start(bf16[3072,128]{1,0:T(8,128)(2,1)S(1)} %gather.12.refs_0_.refs_6_.refs_8_), channel_id=1, source_target_pairs={{0,32},{1,33},{2,34},{3,35},{4,36},{5,37},{6,38},{7,39},{8,40},{9,... | collective-permute-start | bytes 2359304 | tf_op jit(solution)/shard_map/gather/ppermute | solution.py:39
  50.1 20.8 %collective-permute-start.15 = (bf16[3072,128]{1,0:T(8,128)(2,1)S(1)}, bf16[3072,128]{1,0:T(8,128)(2,1)S(1)}, u32[]{:S(2)}, u32[]{:S(2)}) collective-permute-start(bf16[3072,128]{1,0:T(8,128)(2,1)S(1)} %gather.12.refs_0_.refs_6_.refs_8_), channel_id=1, source_target_pairs={{0,96},{1,97},{2,98},{3,99},{4,100},{5,101},{6,102},{7,103},{8,104... | collective-permute-start | bytes 2359304 | tf_op jit(solution)/shard_map/gather/ppermute | solution.py:39
  54.0 5.5 %collective-permute-start.21 = (bf16[32,1152]{1,0:T(8,128)(2,1)S(1)}, bf16[32,1152]{1,0:T(8,128)(2,1)S(1)}, u32[]{:S(2)}, u32[]{:S(2)}) collective-permute-start(bf16[32,1152]{1,0:T(8,128)(2,1)S(1)} %terms.2), channel_id=1, source_target_pairs={{0,1},{1,0},{2,3},{3,2},{4,5},{5,4},{6,7},{7,6},{8,9},{9,8},{10,11... | collective-permute-start | bytes 221192 | tf_op jit(solution)/shard_map/terms/ppermute | solution.py:39
  57.8 17.2 %collective-permute-start.17 = (bf16[528,1024]{1,0:T(8,128)(2,1)S(1)}, bf16[528,1024]{1,0:T(8,128)(2,1)S(1)}, u32[]{:S(2)}, u32[]{:S(2)}) collective-permute-start(bf16[528,1024]{1,0:T(8,128)(2,1)S(1)} %fock.5.refs_2_.refs_0_.refs_1_), channel_id=1, source_target_pairs={{0,8},{1,9},{2,10},{3,11},{4,12},{5,13},{6,14},{7,15},{8,0},{9,1},... | collective-permute-start | bytes 3244040 | tf_op jit(solution)/shard_map/fock/ppermute | solution.py:39
  59.7 29.2 %collective-permute-start.23 = (bf16[528,1024]{1,0:T(8,128)(2,1)S(1)}, bf16[528,1024]{1,0:T(8,128)(2,1)S(1)}, u32[]{:S(2)}, u32[]{:S(2)}) collective-permute-start(bf16[528,1024]{1,0:T(8,128)(2,1)S(1)} %fock.7), channel_id=1, source_target_pairs={{0,1},{1,0},{2,3},{3,2},{4,5},{5,4},{6,7},{7,6},{8,9},{9,8},{10,11... | collective-permute-start | bytes 3244040 | tf_op jit(solution)/shard_map/fock/ppermute | solution.py:39
  63.1 24.7 %collective-permute-start.11 = (bf16[3072,128]{1,0:T(8,128)(2,1)S(1)}, bf16[3072,128]{1,0:T(8,128)(2,1)S(1)}, u32[]{:S(2)}, u32[]{:S(2)}) collective-permute-start(bf16[3072,128]{1,0:T(8,128)(2,1)S(1)} %collective-permute-done.10.refs_1_.refs_3_.refs_5_), channel_id=1, source_target_pairs={{0,32},{1,33},{2,34},{3,35},{4,36},{5,37},{6,38},{7,39},{8,40},{9,... | collective-permute-start | bytes 2359304 | tf_op jit(solution)/shard_map/gather/ppermute | solution.py:39
  71.0 17.9 %collective-permute-start.16 = (bf16[3072,128]{1,0:T(8,128)(2,1)S(1)}, bf16[3072,128]{1,0:T(8,128)(2,1)S(1)}, u32[]{:S(2)}, u32[]{:S(2)}) collective-permute-start(bf16[3072,128]{1,0:T(8,128)(2,1)S(1)} %gather.13), channel_id=1, source_target_pairs={{0,96},{1,97},{2,98},{3,99},{4,100},{5,101},{6,102},{7,103},{8,104... | collective-permute-start | bytes 2359304 | tf_op jit(solution)/shard_map/gather/ppermute | solution.py:39
  73.9 6.1 %collective-permute-start.22 = (bf16[64,1152]{1,0:T(8,128)(2,1)S(1)}, bf16[64,1152]{1,0:T(8,128)(2,1)S(1)}, u32[]{:S(2)}, u32[]{:S(2)}) collective-permute-start(bf16[64,1152]{1,0:T(8,128)(2,1)S(1)} %terms.3.refs_2_), channel_id=1, source_target_pairs={{0,4},{1,5},{2,6},{3,7},{4,0},{5,1},{6,2},{7,3},{8,12},{9,13},{10,... | collective-permute-start | bytes 442376 | tf_op jit(solution)/shard_map/terms/ppermute | solution.py:39
  89.1 6.3 %collective-permute-start.24 = (bf16[528,1024]{1,0:T(8,128)(2,1)S(1)}, bf16[528,1024]{1,0:T(8,128)(2,1)S(1)}, u32[]{:S(2)}, u32[]{:S(2)}) collective-permute-start(bf16[528,1024]{1,0:T(8,128)(2,1)S(1)} %fock.8.refs_0_), channel_id=1, source_target_pairs={{0,8},{1,9},{2,10},{3,11},{4,12},{5,13},{6,14},{7,15},{8,0},{9,1},... | collective-permute-start | bytes 3244040 | tf_op jit(solution)/shard_map/fock/ppermute | solution.py:39
  91.8 13.1 %collective-permute-start.25 = (bf16[1536,128]{1,0:T(8,128)(2,1)S(1)}, bf16[1536,128]{1,0:T(8,128)(2,1)S(1)}, u32[]{:S(2)}, u32[]{:S(2)}) collective-permute-start(bf16[1536,128]{1,0:T(8,128)(2,1)S(1)} %gather.14), channel_id=1, source_target_pairs={{0,16},{1,0},{2,18},{3,2},{4,20},{5,4},{6,22},{7,6},{8,24},{9,8},{... | collective-permute-start | bytes 1179656 | tf_op jit(solution)/shard_map/gather/ppermute | solution.py:39
  94.7 10.2 %collective-permute-start.26 = (bf16[1536,128]{1,0:T(8,128)(2,1)S(1)}, bf16[1536,128]{1,0:T(8,128)(2,1)S(1)}, u32[]{:S(2)}, u32[]{:S(2)}) collective-permute-start(bf16[1536,128]{1,0:T(8,128)(2,1)S(1)} %gather.14), channel_id=1, source_target_pairs={{0,0},{1,16},{2,2},{3,18},{4,4},{5,20},{6,6},{7,22},{8,8},{9,24},{... | collective-permute-start | bytes 1179656 | tf_op jit(solution)/shard_map/gather/ppermute | solution.py:39
  105.3 20.8 %collective-permute-start.27 = (bf16[3072,128]{1,0:T(8,128)(2,1)S(1)}, bf16[3072,128]{1,0:T(8,128)(2,1)S(1)}, u32[]{:S(2)}, u32[]{:S(2)}) collective-permute-start(bf16[3072,128]{1,0:T(8,128)(2,1)S(1)} %gather.15.refs_3_.refs_4_), channel_id=1, source_target_pairs={{0,32},{1,33},{2,34},{3,35},{4,36},{5,37},{6,38},{7,39},{8,40},{9,... | collective-permute-start | bytes 2359304 | tf_op jit(solution)/shard_map/gather/ppermute | solution.py:39
  106.0 20.2 %collective-permute-start.28 = (bf16[3072,128]{1,0:T(8,128)(2,1)S(1)}, bf16[3072,128]{1,0:T(8,128)(2,1)S(1)}, u32[]{:S(2)}, u32[]{:S(2)}) collective-permute-start(bf16[3072,128]{1,0:T(8,128)(2,1)S(1)} %gather.15.refs_3_.refs_4_), channel_id=1, source_target_pairs={{0,96},{1,97},{2,98},{3,99},{4,100},{5,101},{6,102},{7,103},{8,104... | collective-permute-start | bytes 2359304 | tf_op jit(solution)/shard_map/gather/ppermute | solution.py:39
  112.0 11.0 %collective-permute-start.29 = (bf16[768,256]{1,0:T(8,128)(2,1)S(1)}, bf16[768,256]{1,0:T(8,128)(2,1)S(1)}, u32[]{:S(2)}, u32[]{:S(2)}) collective-permute-start(bf16[768,256]{1,0:T(8,128)(2,1)S(1)} %get-tuple-element.36), channel_id=1, source_target_pairs={{0,2},{1,3},{2,4},{3,5},{4,6},{5,7},{6,0},{7,1},{8,10},{9,11},{10,... | collective-permute-start | bytes 1179656 | tf_op jit(solution)/shard_map/reduce/ppermute | solution.py:39
  112.5 10.6 %collective-permute-start.30 = (bf16[768,256]{1,0:T(8,128)(2,1)S(1)}, bf16[768,256]{1,0:T(8,128)(2,1)S(1)}, u32[]{:S(2)}, u32[]{:S(2)}) collective-permute-start(bf16[768,256]{1,0:T(8,128)(2,1)S(1)} %get-tuple-element.35), channel_id=1, source_target_pairs={{0,6},{1,7},{2,0},{3,1},{4,2},{5,3},{6,4},{7,5},{8,14},{9,15},{10,... | collective-permute-start | bytes 1179656 | tf_op jit(solution)/shard_map/reduce/ppermute | solution.py:39
  126.4 19.2 %collective-permute-start.31 = (bf16[1536,256]{1,0:T(8,128)(2,1)S(1)}, bf16[1536,256]{1,0:T(8,128)(2,1)S(1)}, u32[]{:S(2)}, u32[]{:S(2)}) collective-permute-start(bf16[1536,256]{1,0:T(8,128)(2,1)S(1)} %get-tuple-element.25.refs_0_), channel_id=1, source_target_pairs={{0,2},{1,3},{2,4},{3,5},{4,6},{5,7},{6,0},{7,1},{8,10},{9,11},{10,... | collective-permute-start | bytes 2359304 | tf_op jit(solution)/shard_map/reduce/ppermute | solution.py:39
  126.8 18.8 %collective-permute-start.32 = (bf16[1536,256]{1,0:T(8,128)(2,1)S(1)}, bf16[1536,256]{1,0:T(8,128)(2,1)S(1)}, u32[]{:S(2)}, u32[]{:S(2)}) collective-permute-start(bf16[1536,256]{1,0:T(8,128)(2,1)S(1)} %get-tuple-element.26.refs_1_), channel_id=1, source_target_pairs={{0,6},{1,7},{2,0},{3,1},{4,2},{5,3},{6,4},{7,5},{8,14},{9,15},{10,... | collective-permute-start | bytes 2359304 | tf_op jit(solution)/shard_map/reduce/ppermute | solution.py:39
  129.5 10.2 %collective-permute-start.33 = (bf16[1536,128]{1,0:T(8,128)(2,1)S(1)}, bf16[1536,128]{1,0:T(8,128)(2,1)S(1)}, u32[]{:S(2)}, u32[]{:S(2)}) collective-permute-start(bf16[1536,128]{1,0:T(8,128)(2,1)S(1)} %gather.16), channel_id=1, source_target_pairs={{0,32},{1,33},{2,34},{3,35},{4,36},{5,37},{6,38},{7,39},{8,40},{9,... | collective-permute-start | bytes 1179656 | tf_op jit(solution)/shard_map/gather/ppermute | solution.py:39
  130.3 9.4 %collective-permute-start.34 = (bf16[1536,128]{1,0:T(8,128)(2,1)S(1)}, bf16[1536,128]{1,0:T(8,128)(2,1)S(1)}, u32[]{:S(2)}, u32[]{:S(2)}) collective-permute-start(bf16[1536,128]{1,0:T(8,128)(2,1)S(1)} %gather.17), channel_id=1, source_target_pairs={{0,96},{1,97},{2,98},{3,99},{4,100},{5,101},{6,102},{7,103},{8,104... | collective-permute-start | bytes 1179656 | tf_op jit(solution)/shard_map/gather/ppermute | solution.py:39
  142.7 6.3 %collective-permute-start.35 = (bf16[768,128]{1,0:T(8,128)(2,1)S(1)}, bf16[768,128]{1,0:T(8,128)(2,1)S(1)}, u32[]{:S(2)}, u32[]{:S(2)}) collective-permute-start(bf16[768,128]{1,0:T(8,128)(2,1)S(1)} %get-tuple-element.38), channel_id=1, source_target_pairs={{0,2},{1,3},{2,4},{3,5},{4,6},{5,7},{6,0},{7,1},{8,10},{9,11},{10,... | collective-permute-start | bytes 589832 | tf_op jit(solution)/shard_map/reduce/ppermute | solution.py:39
  142.8 6.2 %collective-permute-start.36 = (bf16[768,128]{1,0:T(8,128)(2,1)S(1)}, bf16[768,128]{1,0:T(8,128)(2,1)S(1)}, u32[]{:S(2)}, u32[]{:S(2)}) collective-permute-start(bf16[768,128]{1,0:T(8,128)(2,1)S(1)} %get-tuple-element.37), channel_id=1, source_target_pairs={{0,6},{1,7},{2,0},{3,1},{4,2},{5,3},{6,4},{7,5},{8,14},{9,15},{10,... | collective-permute-start | bytes 589832 | tf_op jit(solution)/shard_map/reduce/ppermute | solution.py:39
  149.1 10.0 %collective-permute-start.37 = (bf16[1536,128]{1,0:T(8,128)(2,1)S(1)}, bf16[1536,128]{1,0:T(8,128)(2,1)S(1)}, u32[]{:S(2)}, u32[]{:S(2)}) collective-permute-start(bf16[1536,128]{1,0:T(8,128)(2,1)S(1)} %get-tuple-element.30.refs_0_), channel_id=1, source_target_pairs={{0,2},{1,3},{2,4},{3,5},{4,6},{5,7},{6,0},{7,1},{8,10},{9,11},{10,... | collective-permute-start | bytes 1179656 | tf_op jit(solution)/shard_map/reduce/ppermute | solution.py:39
  150.4 8.8 %collective-permute-start.38 = (bf16[1536,128]{1,0:T(8,128)(2,1)S(1)}, bf16[1536,128]{1,0:T(8,128)(2,1)S(1)}, u32[]{:S(2)}, u32[]{:S(2)}) collective-permute-start(bf16[1536,128]{1,0:T(8,128)(2,1)S(1)} %get-tuple-element.31.refs_1_), channel_id=1, source_target_pairs={{0,6},{1,7},{2,0},{3,1},{4,2},{5,3},{6,4},{7,5},{8,14},{9,15},{10,... | collective-permute-start | bytes 1179656 | tf_op jit(solution)/shard_map/reduce/ppermute | solution.py:39
  152.1 10.2 %collective-permute-start.39 = (bf16[768,256]{1,0:T(8,128)(2,1)S(1)}, bf16[768,256]{1,0:T(8,128)(2,1)S(1)}, u32[]{:S(2)}, u32[]{:S(2)}) collective-permute-start(bf16[768,256]{1,0:T(8,128)(2,1)S(1)} %get-tuple-element.33), channel_id=1, source_target_pairs={{0,8},{1,9},{2,10},{3,11},{4,12},{5,13},{6,14},{7,15},{8,0},{9,1},... | collective-permute-start | bytes 1179656 | tf_op jit(solution)/shard_map/reduce/ppermute | solution.py:39
  159.3 4.1 %collective-permute-start.40 = (bf16[768,128]{1,0:T(8,128)(2,1)S(1)}, bf16[768,128]{1,0:T(8,128)(2,1)S(1)}, u32[]{:S(2)}, u32[]{:S(2)}) collective-permute-start(bf16[768,128]{1,0:T(8,128)(2,1)S(1)} %get-tuple-element.34), channel_id=1, source_target_pairs={{0,8},{1,9},{2,10},{3,11},{4,12},{5,13},{6,14},{7,15},{8,0},{9,1},... | collective-permute-start | bytes 589832 | tf_op jit(solution)/shard_map/reduce/ppermute | solution.py:39
where the time goes:
time: 166 us
  starting transfers between devices  71 us (43%)
  Pallas kernels  47.8 us (29%)
  waiting for transfers between devices  43.4 us (26%)
  local copies, waits for them, and re-layouts  2.36 us (1%)
    ppermute x37, starting transfers between devices, move(): return lax.ppermute(value, AXES, pairs)  63 us
    pallas_call x29, Pallas kernels, call(): return lambda *operands: run(*after, *operands)  47.8 us
    ppermute x37, waiting for transfers between devices, move(): return lax.ppermute(value, AXES, pairs)  39.8 us
    ppermute x4, starting transfers between devices, shift_row(): return lax.ppermute(value, AXES, pairs)  8.06 us
    ppermute x4, waiting for transfers between devices, shift_row(): return lax.ppermute(value, AXES, pairs)  3.64 us
  transfers between devices with their start and end apart: 41, of which 19 were waited for; matrix products, arithmetic and copies ran while one was open for 1% of the time, Pallas kernels for 27%

commit v1 on v0

--- a/solution.py
+++ b/solution.py
@@ -452,7 +452,8 @@
         ask_above = shift_row(quartet_density, -1)
         ask_below = shift_row(quartet_density, 1)
         pair = jnp.concatenate([density_blocks, swap_yh(density_blocks)], axis=0)
-        moved0 = turned(orbitals, 0, (pair, ask_above, ask_below))
+        piece0 = hold(orbitals[:, :W], (pair, ask_above, ask_below))
+        moved0 = (move_y(piece0, SLOT_A), move_y(piece0, SLOT_B))
         pool = (pair, shift_z(pair, 1), shift_z(pair, -1), shift_z(pair, 2))
         own, for_above, for_below = select((quartet_density, ask_above, ask_below), pool)
         vectors = (own, shift_row(for_above, 1), shift_row(for_below, -1))

time: 166 us -> 165 us (level)
  no operation moved by 1% of the time
where the time goes in v1:
time: 165 us; the launch traced here: 164 us
  starting transfers between devices  71 us (43%)
  Pallas kernels  47.9 us (29%)
  waiting for transfers between devices  42.4 us (26%)
  local copies, waits for them, and re-layouts  2.09 us (1%)
    ppermute x37, starting transfers between devices, move(): return lax.ppermute(value, AXES, pairs)  63 us
    pallas_call x29, Pallas kernels, call(): return lambda *operands: run(*after, *operands)  47.9 us
    ppermute x37, waiting for transfers between devices, move(): return lax.ppermute(value, AXES, pairs)  38.8 us
    ppermute x4, starting transfers between devices, shift_row(): return lax.ppermute(value, AXES, pairs)  8.06 us
    ppermute x4, waiting for transfers between devices, shift_row(): return lax.ppermute(value, AXES, pairs)  3.64 us
  transfers between devices with their start and end apart: 41, of which 19 were waited for; matrix products, arithmetic and copies ran while one was open for 1% of the time, Pallas kernels for 27%

profile of v1, /device:TPU:1, one launch (start us, length us, event | category | flops | bytes accessed | tf_op | source)
XLA Modules:
  0.0 164.5 jit_solution(3012536453390751453)
XLA Ops:
  0.0 1.4 collective-permute-start
  1.4 1.3 collective-permute-start.1
  2.8 2.7 %collective-permute-start.2 = (bf16[40,1024]{1,0:T(8,128)(2,1)}, bf16[40,1024]{1,0:T(8,128)(2,1)S(1)}, u32[]{:S(2)}, u32[]{:S(2)}) collective-permute-start(bf16[40,1024]{1,0:T(8,128)(2,1)} %param.11), channel_id=1, source_target_pairs={{0,1},{1,0},{2,3},{3,2},{4,5},{5,4},{6,7},{7,6},{8,9},{9,8},{10,11... | collective-permute-start | bytes 245768 | tf_op jit(solution)/shard_map/density/ppermute | solution.py:39
  5.5 1.0 slice.21.refs_3_
  6.5 0.9 constant_dynamic-update-slice_fusion.1
  8.0 2.1 %collective-permute-start.8 = (bf16[1536,128]{1,0:T(8,128)(2,1)S(1)}, bf16[1536,128]{1,0:T(8,128)(2,1)S(1)}, u32[]{:S(2)}, u32[]{:S(2)}) collective-permute-start(bf16[1536,128]{1,0:T(8,128)(2,1)S(1)} %density.3), channel_id=1, source_target_pairs={{0,16},{1,0},{2,18},{3,2},{4,20},{5,4},{6,22},{7,6},{8,24},{9,8},{... | collective-permute-start | bytes 1179656 | tf_op jit(solution)/shard_map/density/ppermute | solution.py:39
  10.1 0.7 collective-permute-start.9
  10.8 1.7 %collective-permute-start.3 = (bf16[80,1024]{1,0:T(8,128)(2,1)S(1)}, bf16[80,1024]{1,0:T(8,128)(2,1)S(1)}, u32[]{:S(2)}, u32[]{:S(2)}) collective-permute-start(bf16[80,1024]{1,0:T(8,128)(2,1)S(1)} %constant_dynamic-update-slice_fusion.refs_3_.refs_0_), channel_id=1, source_target_pairs={{0,2},{1,3},{2,4},{3,5},{4,6},{5,7},{6,0},{7,1},{8,10},{9,11},{10,... | collective-permute-start | bytes 491528 | tf_op jit(solution)/shard_map/density/ppermute | solution.py:39
  12.5 2.2 %collective-permute-start.4 = (bf16[80,1024]{1,0:T(8,128)(2,1)S(1)}, bf16[80,1024]{1,0:T(8,128)(2,1)S(1)}, u32[]{:S(2)}, u32[]{:S(2)}) collective-permute-start(bf16[80,1024]{1,0:T(8,128)(2,1)S(1)} %constant_dynamic-update-slice_fusion.refs_3_.refs_0_), channel_id=1, source_target_pairs={{0,6},{1,7},{2,0},{3,1},{4,2},{5,3},{6,4},{7,5},{8,14},{9,15},{10,... | collective-permute-start | bytes 491528 | tf_op jit(solution)/shard_map/density/ppermute | solution.py:39
  14.7 1.2 collective-permute-start.5
  15.9 2.0 %collective-permute-done.3.refs_4_ = bf16[80,1024]{1,0:T(8,128)(2,1)S(1)} collective-permute-done((bf16[80,1024]{1,0:T(8,128)(2,1)S(1)}, bf16[80,1024]{1,0:T(8,128)(2,1)S(1)}, u32[]{:S(2)}, u32[]{:S(2)}) %collective-permute-start.3) | collective-permute-done | bytes 163872 | tf_op jit(solution)/shard_map/density/ppermute | solution.py:39
  17.9 4.5 %collective-permute-done.5.refs_6_ = bf16[80,1024]{1,0:T(8,128)(2,1)S(1)} collective-permute-done((bf16[80,1024]{1,0:T(8,128)(2,1)S(1)}, bf16[80,1024]{1,0:T(8,128)(2,1)S(1)}, u32[]{:S(2)}, u32[]{:S(2)}) %collective-permute-start.5) | collective-permute-done | bytes 163872 | tf_op jit(solution)/shard_map/density/ppermute | solution.py:39
  22.4 0.9 density.2
  23.3 5.3 %collective-permute-start.6 = (bf16[16,1024]{1,0:T(8,128)(2,1)S(1)}, bf16[16,1024]{1,0:T(8,128)(2,1)S(1)}, u32[]{:S(2)}, u32[]{:S(2)}) collective-permute-start(bf16[16,1024]{1,0:T(8,128)(2,1)S(1)} %get-tuple-element.20), channel_id=1, source_target_pairs={{0,8},{1,9},{2,10},{3,11},{4,12},{5,13},{6,14},{7,15},{8,16},{9,17... | collective-permute-start | bytes 98312 | tf_op jit(solution)/shard_map/density/ppermute | solution.py:64
  28.7 1.0 collective-permute-done.6.refs_0_.refs_3_
  29.7 2.6 %collective-permute-done.7.refs_1_.refs_4_ = bf16[16,1024]{1,0:T(8,128)(2,1)S(1)} collective-permute-done((bf16[16,1024]{1,0:T(8,128)(2,1)S(1)}, bf16[16,1024]{1,0:T(8,128)(2,1)S(1)}, u32[]{:S(2)}, u32[]{:S(2)}) %collective-permute-start.7) | collective-permute-done | bytes 32800 | tf_op jit(solution)/shard_map/density/ppermute | solution.py:64
  32.7 0.9 collective-permute-start.10
  33.6 2.5 %collective-permute-start.18 = (bf16[3072,128]{1,0:T(8,128)(2,1)S(1)}, bf16[3072,128]{1,0:T(8,128)(2,1)S(1)}, u32[]{:S(2)}, u32[]{:S(2)}) collective-permute-start(bf16[3072,128]{1,0:T(8,128)(2,1)S(1)} %gather.9.refs_2_.refs_4_), channel_id=1, source_target_pairs={{0,96},{1,97},{2,98},{3,99},{4,100},{5,101},{6,102},{7,103},{8,104... | collective-permute-start | bytes 2359304 | tf_op jit(solution)/shard_map/gather/ppermute | solution.py:39
  36.3 2.0 %collective-permute-start.12 = (bf16[1536,128]{1,0:T(8,128)(2,1)S(1)}, bf16[1536,128]{1,0:T(8,128)(2,1)S(1)}, u32[]{:S(2)}, u32[]{:S(2)}) collective-permute-start(bf16[1536,128]{1,0:T(8,128)(2,1)S(1)} %gather.11), channel_id=1, source_target_pairs={{0,16},{1,0},{2,18},{3,2},{4,20},{5,4},{6,22},{7,6},{8,24},{9,8},{... | collective-permute-start | bytes 1179656 | tf_op jit(solution)/shard_map/gather/ppermute | solution.py:39
  38.3 0.7 collective-permute-start.13
  39.6 7.0 %gather.10.refs_0_ = bf16[8,1152]{1,0:T(8,128)(2,1)S(1)} custom-call(s32[1]{0:T(128)S(6)} %copy.10.refs_0_, s32[8]{0:T(128)S(1)} %copy-done.3, bf16[16,1024]{1,0:T(8,128)(2,1)S(1)} %get-tuple-element.22.refs_2_, bf16[16,1024]{1,0:T(8,128)(2,1)S(1)} %collective-permute-done.6.refs_0_.refs_3_, bf16[16,1024]{1,0:T(8,128)(2,1)S(1)} %collective-permute-done.7.refs_1_.refs_4_, ...), custom_call_target="tpu_custom_call" | custom-call | flops 1 | bytes 1 | tf_op jit(solution)/shard_map/gather/pallas_call | solution.py:90
  46.7 1.2 collective-permute-done.19
  47.9 0.6 collective-permute-start.20
  49.0 2.7 %collective-permute-start.15 = (bf16[3072,128]{1,0:T(8,128)(2,1)S(1)}, bf16[3072,128]{1,0:T(8,128)(2,1)S(1)}, u32[]{:S(2)}, u32[]{:S(2)}) collective-permute-start(bf16[3072,128]{1,0:T(8,128)(2,1)S(1)} %gather.12.refs_0_.refs_6_.refs_8_), channel_id=1, source_target_pairs={{0,96},{1,97},{2,98},{3,99},{4,100},{5,101},{6,102},{7,103},{8,104... | collective-permute-start | bytes 2359304 | tf_op jit(solution)/shard_map/gather/ppermute | solution.py:39
  51.7 1.1 collective-permute-done.10.refs_1_.refs_3_.refs_5_
  52.9 3.8 %collective-permute-start.21 = (bf16[32,1152]{1,0:T(8,128)(2,1)S(1)}, bf16[32,1152]{1,0:T(8,128)(2,1)S(1)}, u32[]{:S(2)}, u32[]{:S(2)}) collective-permute-start(bf16[32,1152]{1,0:T(8,128)(2,1)S(1)} %terms.2), channel_id=1, source_target_pairs={{0,1},{1,0},{2,3},{3,2},{4,5},{5,4},{6,7},{7,6},{8,9},{9,8},{10,11... | collective-permute-start | bytes 221192 | tf_op jit(solution)/shard_map/terms/ppermute | solution.py:39
  56.7 1.3 collective-permute-start.17
  58.0 0.5 collective-permute-done.21
  58.6 3.3 %collective-permute-start.23 = (bf16[528,1024]{1,0:T(8,128)(2,1)S(1)}, bf16[528,1024]{1,0:T(8,128)(2,1)S(1)}, u32[]{:S(2)}, u32[]{:S(2)}) collective-permute-start(bf16[528,1024]{1,0:T(8,128)(2,1)S(1)} %fock.7), channel_id=1, source_target_pairs={{0,1},{1,0},{2,3},{3,2},{4,5},{5,4},{6,7},{7,6},{8,9},{9,8},{10,11... | collective-permute-start | bytes 3244040 | tf_op jit(solution)/shard_map/fock/ppermute | solution.py:39
  61.9 7.9 %collective-permute-done.14.refs_0_.refs_7_.refs_9_ = bf16[3072,128]{1,0:T(8,128)(2,1)S(1)} collective-permute-done((bf16[3072,128]{1,0:T(8,128)(2,1)S(1)}, bf16[3072,128]{1,0:T(8,128)(2,1)S(1)}, u32[]{:S(2)}, u32[]{:S(2)}) %collective-permute-start.14) | collective-permute-done | bytes 786464 | tf_op jit(solution)/shard_map/gather/ppermute | solution.py:39
  69.9 2.7 %collective-permute-start.16 = (bf16[3072,128]{1,0:T(8,128)(2,1)S(1)}, bf16[3072,128]{1,0:T(8,128)(2,1)S(1)}, u32[]{:S(2)}, u32[]{:S(2)}) collective-permute-start(bf16[3072,128]{1,0:T(8,128)(2,1)S(1)} %gather.13), channel_id=1, source_target_pairs={{0,96},{1,97},{2,98},{3,99},{4,100},{5,101},{6,102},{7,103},{8,104... | collective-permute-start | bytes 2359304 | tf_op jit(solution)/shard_map/gather/ppermute | solution.py:39
  72.8 1.1 collective-permute-start.22
  73.9 4.9 %collective-permute-done.22.refs_3_.refs_0_ = bf16[64,1152]{1,0:T(8,128)(2,1)S(1)} collective-permute-done((bf16[64,1152]{1,0:T(8,128)(2,1)S(1)}, bf16[64,1152]{1,0:T(8,128)(2,1)S(1)}, u32[]{:S(2)}, u32[]{:S(2)}) %collective-permute-start.22) | collective-permute-done | bytes 147488 | tf_op jit(solution)/shard_map/terms/ppermute | solution.py:39
  78.8 6.5 %fock.6.refs_0_.refs_2_.refs_1_ = bf16[1536,1536]{1,0:T(8,128)(2,1)S(1)} custom-call(bf16[528,1024]{1,0:T(8,128)(2,1)S(1)} %fock.5.refs_2_.refs_0_.refs_1_, bf16[528,1024]{1,0:T(8,128)(2,1)S(1)} %collective-permute-done.17.refs_1_, bf16[64,1152]{1,0:T(8,128)(2,1)S(1)} %terms.3.refs_2_, bf16[64,1152]{1,0:T(8,128)(2,1)S(1)} %collective-permute-done.22.refs_3_.refs_0_), custom_call_target="tpu_custom_call" | custom-call | flops 1 | bytes 1 | tf_op jit(solution)/shard_map/fock/pallas_call | solution.py:90
  85.4 1.3 collective-permute-done.11.refs_1_.refs_0_.refs_5_.refs_7_
  86.7 1.1 collective-permute-done.16.refs_2_.refs_1_.refs_9_.refs_11_
  87.9 2.7 %collective-permute-start.24 = (bf16[528,1024]{1,0:T(8,128)(2,1)S(1)}, bf16[528,1024]{1,0:T(8,128)(2,1)S(1)}, u32[]{:S(2)}, u32[]{:S(2)}) collective-permute-start(bf16[528,1024]{1,0:T(8,128)(2,1)S(1)} %fock.8.refs_0_), channel_id=1, source_target_pairs={{0,8},{1,9},{2,10},{3,11},{4,12},{5,13},{6,14},{7,15},{8,0},{9,1},... | collective-permute-start | bytes 3244040 | tf_op jit(solution)/shard_map/fock/ppermute | solution.py:39
  90.7 2.9 %collective-permute-start.25 = (bf16[1536,128]{1,0:T(8,128)(2,1)S(1)}, bf16[1536,128]{1,0:T(8,128)(2,1)S(1)}, u32[]{:S(2)}, u32[]{:S(2)}) collective-permute-start(bf16[1536,128]{1,0:T(8,128)(2,1)S(1)} %gather.14), channel_id=1, source_target_pairs={{0,16},{1,0},{2,18},{3,2},{4,20},{5,4},{6,22},{7,6},{8,24},{9,8},{... | collective-permute-start | bytes 1179656 | tf_op jit(solution)/shard_map/gather/ppermute | solution.py:39
  93.6 0.7 collective-permute-start.26
  94.3 6.5 %fock.9.refs_2_.refs_1_.refs_3_ = bf16[1536,1536]{1,0:T(8,128)(2,1)S(1)} custom-call(bf16[528,1024]{1,0:T(8,128)(2,1)S(1)} %fock.8.refs_0_, bf16[528,1024]{1,0:T(8,128)(2,1)S(1)} %collective-permute-done.24.refs_1_, bf16[64,1152]{1,0:T(8,128)(2,1)S(1)} %terms.3.refs_2_, bf16[64,1152]{1,0:T(8,128)(2,1)S(1)} %collective-permute-done.22.refs_3_.refs_0_), custom_call_target="tpu_custom_call" | custom-call | flops 1 | bytes 1 | tf_op jit(solution)/shard_map/fock/pallas_call | solution.py:90
  100.8 3.0 %collective-permute-done.25.refs_3_ = bf16[1536,128]{1,0:T(8,128)(2,1)S(1)} collective-permute-done((bf16[1536,128]{1,0:T(8,128)(2,1)S(1)}, bf16[1536,128]{1,0:T(8,128)(2,1)S(1)}, u32[]{:S(2)}, u32[]{:S(2)}) %collective-permute-start.25) | collective-permute-done | bytes 393248 | tf_op jit(solution)/shard_map/gather/ppermute | solution.py:39
  104.2 0.7 collective-permute-start.27
  104.9 2.9 %collective-permute-start.28 = (bf16[3072,128]{1,0:T(8,128)(2,1)S(1)}, bf16[3072,128]{1,0:T(8,128)(2,1)S(1)}, u32[]{:S(2)}, u32[]{:S(2)}) collective-permute-start(bf16[3072,128]{1,0:T(8,128)(2,1)S(1)} %gather.15.refs_3_.refs_4_), channel_id=1, source_target_pairs={{0,96},{1,97},{2,98},{3,99},{4,100},{5,101},{6,102},{7,103},{8,104... | collective-permute-start | bytes 2359304 | tf_op jit(solution)/shard_map/gather/ppermute | solution.py:39
  107.7 3.0 %reduce.11 = bf16[1536,256]{1,0:T(8,128)(2,1)S(1)} custom-call(bf16[1536,1536]{1,0:T(8,128)(2,1)S(1)} %fock.6.refs_0_.refs_2_.refs_1_, bf16[1536,1536]{1,0:T(8,128)(2,1)S(1)} %fock.9.refs_2_.refs_1_.refs_3_, bf16[3072,128]{1,0:T(8,128)(2,1)S(1)} %gather.9.refs_2_.refs_4_, bf16[3072,128]{1,0:T(8,128)(2,1)S(1)} %collective-permute-done.10.refs_1_.refs_3_.refs_5_, ...), custom_call_target="tpu_custom_call" | custom-call | flops 1 | bytes 1 | tf_op jit(solution)/shard_map/reduce/pallas_call | solution.py:90
  110.8 0.5 collective-permute-start.29
  111.3 2.3 %collective-permute-start.30 = (bf16[768,256]{1,0:T(8,128)(2,1)S(1)}, bf16[768,256]{1,0:T(8,128)(2,1)S(1)}, u32[]{:S(2)}, u32[]{:S(2)}) collective-permute-start(bf16[768,256]{1,0:T(8,128)(2,1)S(1)} %get-tuple-element.35), channel_id=1, source_target_pairs={{0,6},{1,7},{2,0},{3,1},{4,2},{5,3},{6,4},{7,5},{8,14},{9,15},{10,... | collective-permute-start | bytes 1179656 | tf_op jit(solution)/shard_map/reduce/ppermute | solution.py:39
  113.6 6.0 %reduce.10 = (bf16[1536,256]{1,0:T(8,128)(2,1)S(1)}, bf16[1536,256]{1,0:T(8,128)(2,1)S(1)}) custom-call(bf16[1536,1536]{1,0:T(8,128)(2,1)S(1)} %fock.6.refs_0_.refs_2_.refs_1_, bf16[1536,1536]{1,0:T(8,128)(2,1)S(1)} %fock.9.refs_2_.refs_1_.refs_3_, bf16[3072,128]{1,0:T(8,128)(2,1)S(1)} %gather.9.refs_2_.refs_4_, ...), custom_call_target="tpu_custom_call" | custom-call | flops 20000000000 | bytes 1 | tf_op jit(solution)/shard_map/reduce/pallas_call | solution.py:90
  119.6 2.3 %collective-permute-done.29.refs_4_ = bf16[768,256]{1,0:T(8,128)(2,1)S(1)} collective-permute-done((bf16[768,256]{1,0:T(8,128)(2,1)S(1)}, bf16[768,256]{1,0:T(8,128)(2,1)S(1)}, u32[]{:S(2)}, u32[]{:S(2)}) %collective-permute-start.29) | collective-permute-done | bytes 393248 | tf_op jit(solution)/shard_map/reduce/ppermute | solution.py:39
  121.9 3.1 %collective-permute-done.27.refs_0_.refs_4_.refs_5_ = bf16[3072,128]{1,0:T(8,128)(2,1)S(1)} collective-permute-done((bf16[3072,128]{1,0:T(8,128)(2,1)S(1)}, bf16[3072,128]{1,0:T(8,128)(2,1)S(1)}, u32[]{:S(2)}, u32[]{:S(2)}) %collective-permute-start.27) | collective-permute-done | bytes 786464 | tf_op jit(solution)/shard_map/gather/ppermute | solution.py:39
  125.6 2.5 %collective-permute-start.32 = (bf16[1536,256]{1,0:T(8,128)(2,1)S(1)}, bf16[1536,256]{1,0:T(8,128)(2,1)S(1)}, u32[]{:S(2)}, u32[]{:S(2)}) collective-permute-start(bf16[1536,256]{1,0:T(8,128)(2,1)S(1)} %get-tuple-element.26.refs_1_), channel_id=1, source_target_pairs={{0,6},{1,7},{2,0},{3,1},{4,2},{5,3},{6,4},{7,5},{8,14},{9,15},{10,... | collective-permute-start | bytes 2359304 | tf_op jit(solution)/shard_map/reduce/ppermute | solution.py:39
  128.3 0.6 collective-permute-start.33
  129.1 2.2 %collective-permute-start.34 = (bf16[1536,128]{1,0:T(8,128)(2,1)S(1)}, bf16[1536,128]{1,0:T(8,128)(2,1)S(1)}, u32[]{:S(2)}, u32[]{:S(2)}) collective-permute-start(bf16[1536,128]{1,0:T(8,128)(2,1)S(1)} %gather.17), channel_id=1, source_target_pairs={{0,96},{1,97},{2,98},{3,99},{4,100},{5,101},{6,102},{7,103},{8,104... | collective-permute-start | bytes 1179656 | tf_op jit(solution)/shard_map/gather/ppermute | solution.py:39
  131.3 3.0 %reduce.13.refs_0_ = bf16[1536,256]{1,0:T(8,128)(2,1)S(1)} custom-call(bf16[1536,256]{1,0:T(8,128)(2,1)S(1)} %get-tuple-element.25.refs_0_, bf16[1536,256]{1,0:T(8,128)(2,1)S(1)} %get-tuple-element.26.refs_1_, bf16[1536,1536]{1,0:T(8,128)(2,1)S(1)} %fock.6.refs_0_.refs_2_.refs_1_, bf16[1536,1536]{1,0:T(8,128)(2,1)S(1)} %fock.9.refs_2_.refs_1_.refs_3_, ...), custom_call_target="tpu_custom_call" | custom-call | flops 20000000000 | bytes 1 | tf_op jit(solution)/shard_map/reduce/pallas_call | solution.py:90
  134.4 4.1 %collective-permute-done.33.refs_6_.refs_7_ = bf16[1536,128]{1,0:T(8,128)(2,1)S(1)} collective-permute-done((bf16[1536,128]{1,0:T(8,128)(2,1)S(1)}, bf16[1536,128]{1,0:T(8,128)(2,1)S(1)}, u32[]{:S(2)}, u32[]{:S(2)}) %collective-permute-start.33) | collective-permute-done | bytes 393248 | tf_op jit(solution)/shard_map/gather/ppermute | solution.py:39
  138.5 3.0 %reduce.16 = bf16[1536,128]{1,0:T(8,128)(2,1)S(1)} custom-call(bf16[1536,256]{1,0:T(8,128)(2,1)S(1)} %get-tuple-element.25.refs_0_, bf16[1536,256]{1,0:T(8,128)(2,1)S(1)} %get-tuple-element.26.refs_1_, bf16[1536,1536]{1,0:T(8,128)(2,1)S(1)} %fock.6.refs_0_.refs_2_.refs_1_, bf16[1536,1536]{1,0:T(8,128)(2,1)S(1)} %fock.9.refs_2_.refs_1_.refs_3_, ...), custom_call_target="tpu_custom_call" | custom-call | flops 1 | bytes 1 | tf_op jit(solution)/shard_map/reduce/pallas_call | solution.py:90
  141.7 2.7 %collective-permute-start.36 = (bf16[768,128]{1,0:T(8,128)(2,1)S(1)}, bf16[768,128]{1,0:T(8,128)(2,1)S(1)}, u32[]{:S(2)}, u32[]{:S(2)}) collective-permute-start(bf16[768,128]{1,0:T(8,128)(2,1)S(1)} %get-tuple-element.37), channel_id=1, source_target_pairs={{0,6},{1,7},{2,0},{3,1},{4,2},{5,3},{6,4},{7,5},{8,14},{9,15},{10,... | collective-permute-start | bytes 589832 | tf_op jit(solution)/shard_map/reduce/ppermute | solution.py:39
  144.7 3.0 %reduce.15 = (bf16[1536,128]{1,0:T(8,128)(2,1)S(1)}, bf16[1536,128]{1,0:T(8,128)(2,1)S(1)}) custom-call(bf16[768,256]{1,0:T(8,128)(2,1)S(1)} %get-tuple-element.27.refs_0_, bf16[1536,1536]{1,0:T(8,128)(2,1)S(1)} %fock.6.refs_0_.refs_2_.refs_1_, bf16[1536,1536]{1,0:T(8,128)(2,1)S(1)} %fock.9.refs_2_.refs_1_.refs_3_, ...), custom_call_target="tpu_custom_call" | custom-call | flops 20000000000 | bytes 1 | tf_op jit(solution)/shard_map/reduce/pallas_call | solution.py:90
  148.0 1.2 collective-permute-start.37
  149.2 1.7 %collective-permute-start.38 = (bf16[1536,128]{1,0:T(8,128)(2,1)S(1)}, bf16[1536,128]{1,0:T(8,128)(2,1)S(1)}, u32[]{:S(2)}, u32[]{:S(2)}) collective-permute-start(bf16[1536,128]{1,0:T(8,128)(2,1)S(1)} %get-tuple-element.31.refs_1_), channel_id=1, source_target_pairs={{0,6},{1,7},{2,0},{3,1},{4,2},{5,3},{6,4},{7,5},{8,14},{9,15},{10,... | collective-permute-start | bytes 1179656 | tf_op jit(solution)/shard_map/reduce/ppermute | solution.py:39
  150.9 3.7 %collective-permute-start.39 = (bf16[768,256]{1,0:T(8,128)(2,1)S(1)}, bf16[768,256]{1,0:T(8,128)(2,1)S(1)}, u32[]{:S(2)}, u32[]{:S(2)}) collective-permute-start(bf16[768,256]{1,0:T(8,128)(2,1)S(1)} %get-tuple-element.33), channel_id=1, source_target_pairs={{0,8},{1,9},{2,10},{3,11},{4,12},{5,13},{6,14},{7,15},{8,0},{9,1},... | collective-permute-start | bytes 1179656 | tf_op jit(solution)/shard_map/reduce/ppermute | solution.py:39
  154.6 3.3 %reduce.18.refs_0_ = bf16[1536,128]{1,0:T(8,128)(2,1)S(1)} custom-call(bf16[1536,128]{1,0:T(8,128)(2,1)S(1)} %get-tuple-element.30.refs_0_, bf16[1536,128]{1,0:T(8,128)(2,1)S(1)} %get-tuple-element.31.refs_1_, bf16[1536,1536]{1,0:T(8,128)(2,1)S(1)} %fock.6.refs_0_.refs_2_.refs_1_, bf16[1536,1536]{1,0:T(8,128)(2,1)S(1)} %fock.9.refs_2_.refs_1_.refs_3_, ...), custom_call_target="tpu_custom_call" | custom-call | flops 20000000000 | bytes 1 | tf_op jit(solution)/shard_map/reduce/pallas_call | solution.py:90
  158.1 3.0 %collective-permute-start.40 = (bf16[768,128]{1,0:T(8,128)(2,1)S(1)}, bf16[768,128]{1,0:T(8,128)(2,1)S(1)}, u32[]{:S(2)}, u32[]{:S(2)}) collective-permute-start(bf16[768,128]{1,0:T(8,128)(2,1)S(1)} %get-tuple-element.34), channel_id=1, source_target_pairs={{0,8},{1,9},{2,10},{3,11},{4,12},{5,13},{6,14},{7,15},{8,0},{9,1},... | collective-permute-start | bytes 589832 | tf_op jit(solution)/shard_map/reduce/ppermute | solution.py:39
  161.1 1.1 collective-permute-done.40.refs_3_
  162.2 2.3 %finish.1 = bf16[768,768]{1,0:T(8,128)(2,1)} custom-call(bf16[768,256]{1,0:T(8,128)(2,1)S(1)} %get-tuple-element.27.refs_0_, bf16[768,128]{1,0:T(8,128)(2,1)S(1)} %get-tuple-element.32.refs_1_, bf16[768,256]{1,0:T(8,128)(2,1)S(1)} %collective-permute-done.39.refs_2_, bf16[768,128]{1,0:T(8,128)(2,1)S(1)} %collective-permute-done.40.refs_3_), custom_call_target="tpu_custom_call" | custom-call | flops 1 | bytes 1 | tf_op jit(solution)/shard_map/finish/pallas_call | solution.py:90
  (67 shorter events, 4.8 us)
Async XLA Ops:
  0.0 22.4 %copy-start.4 = (s32[8]{0:T(128)S(1)}, s32[8]{0:T(128)}, u32[]{:S(2)}) copy-start(s32[8]{0:T(128)} %refs_0_.3) | copy-start | bytes 100
  0.0 7.8 %collective-permute-start = (s32[8]{0:T(128)}, s32[8]{0:T(128)S(1)}, u32[]{:S(2)}, u32[]{:S(2)}) collective-permute-start(s32[8]{0:T(128)} %refs_0_.3), channel_id=1, source_target_pairs={{0,120},{1,121},{2,122},{3,123},{4,124},{5,125},{6,126},{7,127},{8... | collective-permute-start | bytes 104 | tf_op jit(solution)/shard_map/density/ppermute | solution.py:64
  1.4 6.4 %collective-permute-start.1 = (s32[8]{0:T(128)}, s32[8]{0:T(128)S(1)}, u32[]{:S(2)}, u32[]{:S(2)}) collective-permute-start(s32[8]{0:T(128)} %refs_0_.3), channel_id=1, source_target_pairs={{0,8},{1,9},{2,10},{3,11},{4,12},{5,13},{6,14},{7,15},{8,16},{9,17... | collective-permute-start | bytes 104 | tf_op jit(solution)/shard_map/density/ppermute | solution.py:64
  2.8 5.0 %collective-permute-start.2 = (bf16[40,1024]{1,0:T(8,128)(2,1)}, bf16[40,1024]{1,0:T(8,128)(2,1)S(1)}, u32[]{:S(2)}, u32[]{:S(2)}) collective-permute-start(bf16[40,1024]{1,0:T(8,128)(2,1)} %param.11), channel_id=1, source_target_pairs={{0,1},{1,0},{2,3},{3,2},{4,5},{5,4},{6,7},{7,6},{8,9},{9,8},{10,11... | collective-permute-start | bytes 245768 | tf_op jit(solution)/shard_map/density/ppermute | solution.py:39
  8.0 28.1 %copy-start.1 = (bf16[512,1024]{1,0:T(8,128)(2,1)S(1)}, bf16[512,1024]{1,0:T(8,128)(2,1)}, u32[]{:S(2)}) copy-start(bf16[512,1024]{1,0:T(8,128)(2,1)} %refs_0_.4) | copy-start | bytes 3145732
  8.0 28.1 %copy-start.2 = (s32[512]{0:T(512)S(1)}, s32[512]{0:T(512)}, u32[]{:S(2)}) copy-start(s32[512]{0:T(512)} %param.10) | copy-start | bytes 6148
  8.0 24.3 %collective-permute-start.8 = (bf16[1536,128]{1,0:T(8,128)(2,1)S(1)}, bf16[1536,128]{1,0:T(8,128)(2,1)S(1)}, u32[]{:S(2)}, u32[]{:S(2)}) collective-permute-start(bf16[1536,128]{1,0:T(8,128)(2,1)S(1)} %density.3), channel_id=1, source_target_pairs={{0,16},{1,0},{2,18},{3,2},{4,20},{5,4},{6,22},{7,6},{8,24},{9,8},{... | collective-permute-start | bytes 1179656 | tf_op jit(solution)/shard_map/density/ppermute | solution.py:39
  10.1 22.2 %collective-permute-start.9 = (bf16[1536,128]{1,0:T(8,128)(2,1)S(1)}, bf16[1536,128]{1,0:T(8,128)(2,1)S(1)}, u32[]{:S(2)}, u32[]{:S(2)}) collective-permute-start(bf16[1536,128]{1,0:T(8,128)(2,1)S(1)} %density.3), channel_id=1, source_target_pairs={{0,0},{1,16},{2,2},{3,18},{4,4},{5,20},{6,6},{7,22},{8,8},{9,24},{... | collective-permute-start | bytes 1179656 | tf_op jit(solution)/shard_map/density/ppermute | solution.py:39
  10.8 7.1 %collective-permute-start.3 = (bf16[80,1024]{1,0:T(8,128)(2,1)S(1)}, bf16[80,1024]{1,0:T(8,128)(2,1)S(1)}, u32[]{:S(2)}, u32[]{:S(2)}) collective-permute-start(bf16[80,1024]{1,0:T(8,128)(2,1)S(1)} %constant_dynamic-update-slice_fusion.refs_3_.refs_0_), channel_id=1, source_target_pairs={{0,2},{1,3},{2,4},{3,5},{4,6},{5,7},{6,0},{7,1},{8,10},{9,11},{10,... | collective-permute-start | bytes 491528 | tf_op jit(solution)/shard_map/density/ppermute | solution.py:39
  12.5 5.4 %collective-permute-start.4 = (bf16[80,1024]{1,0:T(8,128)(2,1)S(1)}, bf16[80,1024]{1,0:T(8,128)(2,1)S(1)}, u32[]{:S(2)}, u32[]{:S(2)}) collective-permute-start(bf16[80,1024]{1,0:T(8,128)(2,1)S(1)} %constant_dynamic-update-slice_fusion.refs_3_.refs_0_), channel_id=1, source_target_pairs={{0,6},{1,7},{2,0},{3,1},{4,2},{5,3},{6,4},{7,5},{8,14},{9,15},{10,... | collective-permute-start | bytes 491528 | tf_op jit(solution)/shard_map/density/ppermute | solution.py:39
  14.7 7.7 %collective-permute-start.5 = (bf16[80,1024]{1,0:T(8,128)(2,1)S(1)}, bf16[80,1024]{1,0:T(8,128)(2,1)S(1)}, u32[]{:S(2)}, u32[]{:S(2)}) collective-permute-start(bf16[80,1024]{1,0:T(8,128)(2,1)S(1)} %constant_dynamic-update-slice_fusion.refs_3_.refs_0_), channel_id=1, source_target_pairs={{0,4},{1,5},{2,6},{3,7},{4,0},{5,1},{6,2},{7,3},{8,12},{9,13},{10,... | collective-permute-start | bytes 491528 | tf_op jit(solution)/shard_map/density/ppermute | solution.py:39
  23.3 6.3 %collective-permute-start.6 = (bf16[16,1024]{1,0:T(8,128)(2,1)S(1)}, bf16[16,1024]{1,0:T(8,128)(2,1)S(1)}, u32[]{:S(2)}, u32[]{:S(2)}) collective-permute-start(bf16[16,1024]{1,0:T(8,128)(2,1)S(1)} %get-tuple-element.20), channel_id=1, source_target_pairs={{0,8},{1,9},{2,10},{3,11},{4,12},{5,13},{6,14},{7,15},{8,16},{9,17... | collective-permute-start | bytes 98312 | tf_op jit(solution)/shard_map/density/ppermute | solution.py:64
  28.7 3.6 %collective-permute-start.7 = (bf16[16,1024]{1,0:T(8,128)(2,1)S(1)}, bf16[16,1024]{1,0:T(8,128)(2,1)S(1)}, u32[]{:S(2)}, u32[]{:S(2)}) collective-permute-start(bf16[16,1024]{1,0:T(8,128)(2,1)S(1)} %get-tuple-element.21), channel_id=1, source_target_pairs={{0,120},{1,121},{2,122},{3,123},{4,124},{5,125},{6,126},{7,127},{8... | collective-permute-start | bytes 98312 | tf_op jit(solution)/shard_map/density/ppermute | solution.py:64
  32.7 3.5 %copy-start = (bf16[1536,384]{1,0:T(8,128)(2,1)S(1)}, bf16[1536,384]{1,0:T(8,128)(2,1)}, u32[]{:S(2)}) copy-start(bf16[1536,384]{1,0:T(8,128)(2,1)} %refs_1_.3) | copy-start | bytes 3538948
  32.7 20.1 %collective-permute-start.10 = (bf16[3072,128]{1,0:T(8,128)(2,1)S(1)}, bf16[3072,128]{1,0:T(8,128)(2,1)S(1)}, u32[]{:S(2)}, u32[]{:S(2)}) collective-permute-start(bf16[3072,128]{1,0:T(8,128)(2,1)S(1)} %gather.9.refs_2_.refs_4_), channel_id=1, source_target_pairs={{0,32},{1,33},{2,34},{3,35},{4,36},{5,37},{6,38},{7,39},{8,40},{9,... | collective-permute-start | bytes 2359304 | tf_op jit(solution)/shard_map/gather/ppermute | solution.py:39
  33.6 19.2 %collective-permute-start.18 = (bf16[3072,128]{1,0:T(8,128)(2,1)S(1)}, bf16[3072,128]{1,0:T(8,128)(2,1)S(1)}, u32[]{:S(2)}, u32[]{:S(2)}) collective-permute-start(bf16[3072,128]{1,0:T(8,128)(2,1)S(1)} %gather.9.refs_2_.refs_4_), channel_id=1, source_target_pairs={{0,96},{1,97},{2,98},{3,99},{4,100},{5,101},{6,102},{7,103},{8,104... | collective-permute-start | bytes 2359304 | tf_op jit(solution)/shard_map/gather/ppermute | solution.py:39
  36.2 3.4 %copy-start.3 = (s32[8]{0:T(128)S(1)}, s32[8]{0:T(128)}, u32[]{:S(2)}) copy-start(s32[8]{0:T(128)} %refs_1_.2) | copy-start | bytes 100
  36.3 12.2 %collective-permute-start.12 = (bf16[1536,128]{1,0:T(8,128)(2,1)S(1)}, bf16[1536,128]{1,0:T(8,128)(2,1)S(1)}, u32[]{:S(2)}, u32[]{:S(2)}) collective-permute-start(bf16[1536,128]{1,0:T(8,128)(2,1)S(1)} %gather.11), channel_id=1, source_target_pairs={{0,16},{1,0},{2,18},{3,2},{4,20},{5,4},{6,22},{7,6},{8,24},{9,8},{... | collective-permute-start | bytes 1179656 | tf_op jit(solution)/shard_map/gather/ppermute | solution.py:39
  38.3 10.2 %collective-permute-start.13 = (bf16[1536,128]{1,0:T(8,128)(2,1)S(1)}, bf16[1536,128]{1,0:T(8,128)(2,1)S(1)}, u32[]{:S(2)}, u32[]{:S(2)}) collective-permute-start(bf16[1536,128]{1,0:T(8,128)(2,1)S(1)} %gather.11), channel_id=1, source_target_pairs={{0,0},{1,16},{2,2},{3,18},{4,4},{5,20},{6,6},{7,22},{8,8},{9,24},{... | collective-permute-start | bytes 1179656 | tf_op jit(solution)/shard_map/gather/ppermute | solution.py:39
  46.6 1.3 collective-permute-start.19
  47.9 3.8 %collective-permute-start.20 = (bf16[16,1152]{1,0:T(8,128)(2,1)S(1)}, bf16[16,1152]{1,0:T(8,128)(2,1)S(1)}, u32[]{:S(2)}, u32[]{:S(2)}) collective-permute-start(bf16[16,1152]{1,0:T(8,128)(2,1)S(1)} %pad_maximum_fusion.2), channel_id=1, source_target_pairs={{0,2},{1,3},{2,0},{3,1},{4,6},{5,7},{6,4},{7,5},{8,10},{9,11},{10,... | collective-permute-start | bytes 110600 | tf_op jit(solution)/shard_map/terms/ppermute | solution.py:39
  48.9 20.9 %collective-permute-start.14 = (bf16[3072,128]{1,0:T(8,128)(2,1)S(1)}, bf16[3072,128]{1,0:T(8,128)(2,1)S(1)}, u32[]{:S(2)}, u32[]{:S(2)}) collective-permute-start(bf16[3072,128]{1,0:T(8,128)(2,1)S(1)} %gather.12.refs_0_.refs_6_.refs_8_), channel_id=1, source_target_pairs={{0,32},{1,33},{2,34},{3,35},{4,36},{5,37},{6,38},{7,39},{8,40},{9,... | collective-permute-start | bytes 2359304 | tf_op jit(solution)/shard_map/gather/ppermute | solution.py:39
  49.0 20.8 %collective-permute-start.15 = (bf16[3072,128]{1,0:T(8,128)(2,1)S(1)}, bf16[3072,128]{1,0:T(8,128)(2,1)S(1)}, u32[]{:S(2)}, u32[]{:S(2)}) collective-permute-start(bf16[3072,128]{1,0:T(8,128)(2,1)S(1)} %gather.12.refs_0_.refs_6_.refs_8_), channel_id=1, source_target_pairs={{0,96},{1,97},{2,98},{3,99},{4,100},{5,101},{6,102},{7,103},{8,104... | collective-permute-start | bytes 2359304 | tf_op jit(solution)/shard_map/gather/ppermute | solution.py:39
  52.9 5.5 %collective-permute-start.21 = (bf16[32,1152]{1,0:T(8,128)(2,1)S(1)}, bf16[32,1152]{1,0:T(8,128)(2,1)S(1)}, u32[]{:S(2)}, u32[]{:S(2)}) collective-permute-start(bf16[32,1152]{1,0:T(8,128)(2,1)S(1)} %terms.2), channel_id=1, source_target_pairs={{0,1},{1,0},{2,3},{3,2},{4,5},{5,4},{6,7},{7,6},{8,9},{9,8},{10,11... | collective-permute-start | bytes 221192 | tf_op jit(solution)/shard_map/terms/ppermute | solution.py:39
  56.7 17.2 %collective-permute-start.17 = (bf16[528,1024]{1,0:T(8,128)(2,1)S(1)}, bf16[528,1024]{1,0:T(8,128)(2,1)S(1)}, u32[]{:S(2)}, u32[]{:S(2)}) collective-permute-start(bf16[528,1024]{1,0:T(8,128)(2,1)S(1)} %fock.5.refs_2_.refs_0_.refs_1_), channel_id=1, source_target_pairs={{0,8},{1,9},{2,10},{3,11},{4,12},{5,13},{6,14},{7,15},{8,0},{9,1},... | collective-permute-start | bytes 3244040 | tf_op jit(solution)/shard_map/fock/ppermute | solution.py:39
  58.6 29.2 %collective-permute-start.23 = (bf16[528,1024]{1,0:T(8,128)(2,1)S(1)}, bf16[528,1024]{1,0:T(8,128)(2,1)S(1)}, u32[]{:S(2)}, u32[]{:S(2)}) collective-permute-start(bf16[528,1024]{1,0:T(8,128)(2,1)S(1)} %fock.7), channel_id=1, source_target_pairs={{0,1},{1,0},{2,3},{3,2},{4,5},{5,4},{6,7},{7,6},{8,9},{9,8},{10,11... | collective-permute-start | bytes 3244040 | tf_op jit(solution)/shard_map/fock/ppermute | solution.py:39
  61.9 24.7 %collective-permute-start.11 = (bf16[3072,128]{1,0:T(8,128)(2,1)S(1)}, bf16[3072,128]{1,0:T(8,128)(2,1)S(1)}, u32[]{:S(2)}, u32[]{:S(2)}) collective-permute-start(bf16[3072,128]{1,0:T(8,128)(2,1)S(1)} %collective-permute-done.10.refs_1_.refs_3_.refs_5_), channel_id=1, source_target_pairs={{0,32},{1,33},{2,34},{3,35},{4,36},{5,37},{6,38},{7,39},{8,40},{9,... | collective-permute-start | bytes 2359304 | tf_op jit(solution)/shard_map/gather/ppermute | solution.py:39
  69.9 17.9 %collective-permute-start.16 = (bf16[3072,128]{1,0:T(8,128)(2,1)S(1)}, bf16[3072,128]{1,0:T(8,128)(2,1)S(1)}, u32[]{:S(2)}, u32[]{:S(2)}) collective-permute-start(bf16[3072,128]{1,0:T(8,128)(2,1)S(1)} %gather.13), channel_id=1, source_target_pairs={{0,96},{1,97},{2,98},{3,99},{4,100},{5,101},{6,102},{7,103},{8,104... | collective-permute-start | bytes 2359304 | tf_op jit(solution)/shard_map/gather/ppermute | solution.py:39
  72.8 6.1 %collective-permute-start.22 = (bf16[64,1152]{1,0:T(8,128)(2,1)S(1)}, bf16[64,1152]{1,0:T(8,128)(2,1)S(1)}, u32[]{:S(2)}, u32[]{:S(2)}) collective-permute-start(bf16[64,1152]{1,0:T(8,128)(2,1)S(1)} %terms.3.refs_2_), channel_id=1, source_target_pairs={{0,4},{1,5},{2,6},{3,7},{4,0},{5,1},{6,2},{7,3},{8,12},{9,13},{10,... | collective-permute-start | bytes 442376 | tf_op jit(solution)/shard_map/terms/ppermute | solution.py:39
  87.9 6.3 %collective-permute-start.24 = (bf16[528,1024]{1,0:T(8,128)(2,1)S(1)}, bf16[528,1024]{1,0:T(8,128)(2,1)S(1)}, u32[]{:S(2)}, u32[]{:S(2)}) collective-permute-start(bf16[528,1024]{1,0:T(8,128)(2,1)S(1)} %fock.8.refs_0_), channel_id=1, source_target_pairs={{0,8},{1,9},{2,10},{3,11},{4,12},{5,13},{6,14},{7,15},{8,0},{9,1},... | collective-permute-start | bytes 3244040 | tf_op jit(solution)/shard_map/fock/ppermute | solution.py:39
  90.7 13.1 %collective-permute-start.25 = (bf16[1536,128]{1,0:T(8,128)(2,1)S(1)}, bf16[1536,128]{1,0:T(8,128)(2,1)S(1)}, u32[]{:S(2)}, u32[]{:S(2)}) collective-permute-start(bf16[1536,128]{1,0:T(8,128)(2,1)S(1)} %gather.14), channel_id=1, source_target_pairs={{0,16},{1,0},{2,18},{3,2},{4,20},{5,4},{6,22},{7,6},{8,24},{9,8},{... | collective-permute-start | bytes 1179656 | tf_op jit(solution)/shard_map/gather/ppermute | solution.py:39
  93.6 10.2 %collective-permute-start.26 = (bf16[1536,128]{1,0:T(8,128)(2,1)S(1)}, bf16[1536,128]{1,0:T(8,128)(2,1)S(1)}, u32[]{:S(2)}, u32[]{:S(2)}) collective-permute-start(bf16[1536,128]{1,0:T(8,128)(2,1)S(1)} %gather.14), channel_id=1, source_target_pairs={{0,0},{1,16},{2,2},{3,18},{4,4},{5,20},{6,6},{7,22},{8,8},{9,24},{... | collective-permute-start | bytes 1179656 | tf_op jit(solution)/shard_map/gather/ppermute | solution.py:39
  104.2 20.8 %collective-permute-start.27 = (bf16[3072,128]{1,0:T(8,128)(2,1)S(1)}, bf16[3072,128]{1,0:T(8,128)(2,1)S(1)}, u32[]{:S(2)}, u32[]{:S(2)}) collective-permute-start(bf16[3072,128]{1,0:T(8,128)(2,1)S(1)} %gather.15.refs_3_.refs_4_), channel_id=1, source_target_pairs={{0,32},{1,33},{2,34},{3,35},{4,36},{5,37},{6,38},{7,39},{8,40},{9,... | collective-permute-start | bytes 2359304 | tf_op jit(solution)/shard_map/gather/ppermute | solution.py:39
  104.9 20.2 %collective-permute-start.28 = (bf16[3072,128]{1,0:T(8,128)(2,1)S(1)}, bf16[3072,128]{1,0:T(8,128)(2,1)S(1)}, u32[]{:S(2)}, u32[]{:S(2)}) collective-permute-start(bf16[3072,128]{1,0:T(8,128)(2,1)S(1)} %gather.15.refs_3_.refs_4_), channel_id=1, source_target_pairs={{0,96},{1,97},{2,98},{3,99},{4,100},{5,101},{6,102},{7,103},{8,104... | collective-permute-start | bytes 2359304 | tf_op jit(solution)/shard_map/gather/ppermute | solution.py:39
  110.8 11.0 %collective-permute-start.29 = (bf16[768,256]{1,0:T(8,128)(2,1)S(1)}, bf16[768,256]{1,0:T(8,128)(2,1)S(1)}, u32[]{:S(2)}, u32[]{:S(2)}) collective-permute-start(bf16[768,256]{1,0:T(8,128)(2,1)S(1)} %get-tuple-element.36), channel_id=1, source_target_pairs={{0,2},{1,3},{2,4},{3,5},{4,6},{5,7},{6,0},{7,1},{8,10},{9,11},{10,... | collective-permute-start | bytes 1179656 | tf_op jit(solution)/shard_map/reduce/ppermute | solution.py:39
  111.3 10.6 %collective-permute-start.30 = (bf16[768,256]{1,0:T(8,128)(2,1)S(1)}, bf16[768,256]{1,0:T(8,128)(2,1)S(1)}, u32[]{:S(2)}, u32[]{:S(2)}) collective-permute-start(bf16[768,256]{1,0:T(8,128)(2,1)S(1)} %get-tuple-element.35), channel_id=1, source_target_pairs={{0,6},{1,7},{2,0},{3,1},{4,2},{5,3},{6,4},{7,5},{8,14},{9,15},{10,... | collective-permute-start | bytes 1179656 | tf_op jit(solution)/shard_map/reduce/ppermute | solution.py:39
  125.2 19.2 %collective-permute-start.31 = (bf16[1536,256]{1,0:T(8,128)(2,1)S(1)}, bf16[1536,256]{1,0:T(8,128)(2,1)S(1)}, u32[]{:S(2)}, u32[]{:S(2)}) collective-permute-start(bf16[1536,256]{1,0:T(8,128)(2,1)S(1)} %get-tuple-element.25.refs_0_), channel_id=1, source_target_pairs={{0,2},{1,3},{2,4},{3,5},{4,6},{5,7},{6,0},{7,1},{8,10},{9,11},{10,... | collective-permute-start | bytes 2359304 | tf_op jit(solution)/shard_map/reduce/ppermute | solution.py:39
  125.6 18.8 %collective-permute-start.32 = (bf16[1536,256]{1,0:T(8,128)(2,1)S(1)}, bf16[1536,256]{1,0:T(8,128)(2,1)S(1)}, u32[]{:S(2)}, u32[]{:S(2)}) collective-permute-start(bf16[1536,256]{1,0:T(8,128)(2,1)S(1)} %get-tuple-element.26.refs_1_), channel_id=1, source_target_pairs={{0,6},{1,7},{2,0},{3,1},{4,2},{5,3},{6,4},{7,5},{8,14},{9,15},{10,... | collective-permute-start | bytes 2359304 | tf_op jit(solution)/shard_map/reduce/ppermute | solution.py:39
  128.3 10.2 %collective-permute-start.33 = (bf16[1536,128]{1,0:T(8,128)(2,1)S(1)}, bf16[1536,128]{1,0:T(8,128)(2,1)S(1)}, u32[]{:S(2)}, u32[]{:S(2)}) collective-permute-start(bf16[1536,128]{1,0:T(8,128)(2,1)S(1)} %gather.16), channel_id=1, source_target_pairs={{0,32},{1,33},{2,34},{3,35},{4,36},{5,37},{6,38},{7,39},{8,40},{9,... | collective-permute-start | bytes 1179656 | tf_op jit(solution)/shard_map/gather/ppermute | solution.py:39
  129.1 9.4 %collective-permute-start.34 = (bf16[1536,128]{1,0:T(8,128)(2,1)S(1)}, bf16[1536,128]{1,0:T(8,128)(2,1)S(1)}, u32[]{:S(2)}, u32[]{:S(2)}) collective-permute-start(bf16[1536,128]{1,0:T(8,128)(2,1)S(1)} %gather.17), channel_id=1, source_target_pairs={{0,96},{1,97},{2,98},{3,99},{4,100},{5,101},{6,102},{7,103},{8,104... | collective-permute-start | bytes 1179656 | tf_op jit(solution)/shard_map/gather/ppermute | solution.py:39
  141.6 6.3 %collective-permute-start.35 = (bf16[768,128]{1,0:T(8,128)(2,1)S(1)}, bf16[768,128]{1,0:T(8,128)(2,1)S(1)}, u32[]{:S(2)}, u32[]{:S(2)}) collective-permute-start(bf16[768,128]{1,0:T(8,128)(2,1)S(1)} %get-tuple-element.38), channel_id=1, source_target_pairs={{0,2},{1,3},{2,4},{3,5},{4,6},{5,7},{6,0},{7,1},{8,10},{9,11},{10,... | collective-permute-start | bytes 589832 | tf_op jit(solution)/shard_map/reduce/ppermute | solution.py:39
  141.7 6.2 %collective-permute-start.36 = (bf16[768,128]{1,0:T(8,128)(2,1)S(1)}, bf16[768,128]{1,0:T(8,128)(2,1)S(1)}, u32[]{:S(2)}, u32[]{:S(2)}) collective-permute-start(bf16[768,128]{1,0:T(8,128)(2,1)S(1)} %get-tuple-element.37), channel_id=1, source_target_pairs={{0,6},{1,7},{2,0},{3,1},{4,2},{5,3},{6,4},{7,5},{8,14},{9,15},{10,... | collective-permute-start | bytes 589832 | tf_op jit(solution)/shard_map/reduce/ppermute | solution.py:39
  148.0 10.0 %collective-permute-start.37 = (bf16[1536,128]{1,0:T(8,128)(2,1)S(1)}, bf16[1536,128]{1,0:T(8,128)(2,1)S(1)}, u32[]{:S(2)}, u32[]{:S(2)}) collective-permute-start(bf16[1536,128]{1,0:T(8,128)(2,1)S(1)} %get-tuple-element.30.refs_0_), channel_id=1, source_target_pairs={{0,2},{1,3},{2,4},{3,5},{4,6},{5,7},{6,0},{7,1},{8,10},{9,11},{10,... | collective-permute-start | bytes 1179656 | tf_op jit(solution)/shard_map/reduce/ppermute | solution.py:39
  149.2 8.8 %collective-permute-start.38 = (bf16[1536,128]{1,0:T(8,128)(2,1)S(1)}, bf16[1536,128]{1,0:T(8,128)(2,1)S(1)}, u32[]{:S(2)}, u32[]{:S(2)}) collective-permute-start(bf16[1536,128]{1,0:T(8,128)(2,1)S(1)} %get-tuple-element.31.refs_1_), channel_id=1, source_target_pairs={{0,6},{1,7},{2,0},{3,1},{4,2},{5,3},{6,4},{7,5},{8,14},{9,15},{10,... | collective-permute-start | bytes 1179656 | tf_op jit(solution)/shard_map/reduce/ppermute | solution.py:39
  150.9 10.2 %collective-permute-start.39 = (bf16[768,256]{1,0:T(8,128)(2,1)S(1)}, bf16[768,256]{1,0:T(8,128)(2,1)S(1)}, u32[]{:S(2)}, u32[]{:S(2)}) collective-permute-start(bf16[768,256]{1,0:T(8,128)(2,1)S(1)} %get-tuple-element.33), channel_id=1, source_target_pairs={{0,8},{1,9},{2,10},{3,11},{4,12},{5,13},{6,14},{7,15},{8,0},{9,1},... | collective-permute-start | bytes 1179656 | tf_op jit(solution)/shard_map/reduce/ppermute | solution.py:39
  158.1 4.1 %collective-permute-start.40 = (bf16[768,128]{1,0:T(8,128)(2,1)S(1)}, bf16[768,128]{1,0:T(8,128)(2,1)S(1)}, u32[]{:S(2)}, u32[]{:S(2)}) collective-permute-start(bf16[768,128]{1,0:T(8,128)(2,1)S(1)} %get-tuple-element.34), channel_id=1, source_target_pairs={{0,8},{1,9},{2,10},{3,11},{4,12},{5,13},{6,14},{7,15},{8,0},{9,1},... | collective-permute-start | bytes 589832 | tf_op jit(solution)/shard_map/reduce/ppermute | solution.py:39
